TPU v7x, 256 devices: a whole 4x4x8 slice. The times are simulated.
256 devices in a mesh: sy: 8 (over y, x_lo), sx: 16 (over z, core), dp: 2 (over x_hi).
Axes of the slice: x: 4 (x_hi: 2, x_lo: 2; x = x_hi * 2 + x_lo), y: 4, z: 8, core: 2. Of those that a mesh axis runs over, the one named last changes fastest.
Arguments:
- tokens: bfloat16 [2, 128, 512, 512], P('dp', 'sy', 'sx'), may hold values from -6 to 6
- cotangent: bfloat16 [2, 128, 512, 512], P('dp', 'sy', 'sx'), may hold values from -6 to 6
- w_qkv: bfloat16 [512, 1536], replicated, may hold values from -0.25 to 0.25
- w_proj: bfloat16 [512, 512], replicated, may hold values from -0.25 to 0.25
- logit_scale: float32 [16], replicated, may hold values from 2 to 20
- w_router: bfloat16 [512, 32], replicated, may hold values from -0.25 to 0.25
- w_up: bfloat16 [32, 512, 2048], P('sx'), may hold values from -0.25 to 0.25
- w_down: bfloat16 [32, 2048, 512], P('sx'), may hold values from -0.125 to 0.125
- expert_ids: int32 [2, 8, 16, 512, 1], P('dp', 'sy', 'sx'), may hold values from 0 to 31; in each aligned block of 512 rows (0 to 511, 512 to 1023, ..., all dimensions but the last counted through in order) at most 32 rows name the same one
Outputs:
- mixed: bfloat16 [2, 128, 512, 512], P('dp', 'sy', 'sx')
- grad_up: float32 [32, 512, 2048], P('sx', None, ('sy', 'dp'))
- grad_down: float32 [32, 2048, 512], P('sx', ('sy', 'dp'))
Inputs may be any that keep to these rules, and one draw needn't show every extreme that they name: `expert_ids`: among the tokens of one device no expert is named by more than 32 tokens.
All inputs are finite; a program needn't handle non-finite values.
Results may differ from a plain program's by a relative error of at most 0.024.
Values may be sent and summed in bfloat16 or wider, within the bound.
A program may use at most 128 MiB of HBM per device.

v0:
```python
import jax
import jax.numpy as jnp
from jax import lax
from jax.sharding import PartitionSpec as P

WIN = 16
SHIFT = 8


def from_behind(block, axis, distance):
    devices = range(lax.axis_size(axis))
    route = [((i - distance) % len(devices), i) for i in devices]
    return lax.ppermute(block, axis, route)


def layer_norm(values_in):
    mean = jnp.mean(values_in, axis=-1, keepdims=True)
    centred = values_in - mean
    return centred * lax.rsqrt(jnp.mean(centred * centred, axis=-1, keepdims=True) + 1e-05)


def attend(windows, labels, w_qkv, w_proj, logit_scale):
    count, length, width = windows.shape
    heads = logit_scale.shape[0]
    head_dim = width // heads
    normed = layer_norm(windows.astype(jnp.float32)).astype(jnp.bfloat16)
    mixed = jnp.dot(
        normed.reshape(count * length, width), w_qkv, preferred_element_type=jnp.float32
    )
    mixed = mixed.reshape(count, length, 3, heads, head_dim)
    query = mixed[:, :, 0]
    keys = mixed[:, :, 1]
    values = mixed[:, :, 2].astype(jnp.bfloat16)
    query = query / jnp.maximum(jnp.sqrt(jnp.sum(query * query, axis=-1, keepdims=True)), 4.0)
    keys = keys / jnp.maximum(jnp.sqrt(jnp.sum(keys * keys, axis=-1, keepdims=True)), 4.0)
    scores = jnp.einsum("wqhc,wkhc->whqk", query, keys, precision=lax.Precision.HIGHEST)
    scores = scores * logit_scale[None, :, None, None]
    allowed = labels[:, None, :, None] == labels[:, None, None, :]
    weights = jnp.where(allowed, jnp.exp(scores), 0.0)
    probs = (weights / jnp.sum(weights, axis=-1, keepdims=True)).astype(jnp.bfloat16)
    joined = jnp.einsum("whqk,wkhc->wqhc", probs, values, preferred_element_type=jnp.float32)
    joined = joined.astype(jnp.bfloat16).reshape(count * length, width)
    result = jnp.dot(joined, w_proj, preferred_element_type=jnp.float32).astype(jnp.bfloat16)
    return result.reshape(count, length, width)


def expert_grads(rows_in, rows_grad, act, hidden, w_down_part):
    grad_down_e = jnp.einsum(
        "secf,secd->efd", hidden, rows_grad, preferred_element_type=jnp.float32
    )
    grad_hidden = jnp.einsum(
        "secd,efd->secf", rows_grad, w_down_part, preferred_element_type=jnp.float32
    )
    grad_act = jax.vjp(jax.nn.gelu, act)[1](grad_hidden)[0].astype(jnp.bfloat16)
    grad_up_e = jnp.einsum("secd,secf->edf", rows_in, grad_act, preferred_element_type=jnp.float32)
    return (grad_up_e, grad_down_e)


def on_device(tokens, cotangent, w_qkv, w_proj, logit_scale, w_router, w_up, w_down, expert_ids):
    tile = tokens[0]
    rows_t, cols_t, width = tile.shape
    upper = from_behind(tile[rows_t - SHIFT :], "sy", 1)
    row_moved = jnp.concatenate([upper, tile[: rows_t - SHIFT]], 0)
    left = from_behind(row_moved[:, cols_t - SHIFT :], "sx", 1)
    region = jnp.concatenate([left, row_moved[:, : cols_t - SHIFT]], 1)
    row_label = jnp.where((lax.axis_index("sy") == 0) & (jnp.arange(rows_t) >= SHIFT), 1, 0).astype(
        jnp.int32
    )
    col_label = jnp.where((lax.axis_index("sx") == 0) & (jnp.arange(cols_t) >= SHIFT), 1, 0).astype(
        jnp.int32
    )
    label_map = row_label[:, None] * 2 + col_label[None, :]
    rows_h = rows_t // WIN
    cols_w = cols_t // WIN
    length = WIN * WIN
    windows = (
        region.reshape(rows_h, WIN, cols_w, WIN, width)
        .transpose(0, 2, 1, 3, 4)
        .reshape(rows_h * cols_w, length, width)
    )
    labels = (
        label_map.reshape(rows_h, WIN, cols_w, WIN)
        .transpose(0, 2, 1, 3)
        .reshape(rows_h * cols_w, length)
    )
    attended = attend(windows, labels, w_qkv, w_proj, logit_scale)
    attended = (
        attended.reshape(rows_h, cols_w, WIN, WIN, width)
        .transpose(0, 2, 1, 3, 4)
        .reshape(rows_t, cols_t, width)
    )
    right = from_behind(attended[:, :SHIFT], "sx", -1)
    col_home = jnp.concatenate([attended[:, SHIFT:], right], 1)
    lower = from_behind(col_home[:SHIFT], "sy", -1)
    attn_home = jnp.concatenate([col_home[SHIFT:], lower], 0)
    count_tok = rows_t * cols_t
    resid = (tile.astype(jnp.float32) + attn_home.astype(jnp.float32)).reshape(count_tok, width)
    normed = layer_norm(resid).astype(jnp.bfloat16)
    experts_all = w_router.shape[1]
    exp_dev = w_up.shape[0]
    n_sx = lax.axis_size("sx")
    cap = 2 * count_tok // experts_all
    slots = experts_all * cap
    ids = expert_ids.reshape(count_tok)
    logits = jnp.dot(normed, w_router, preferred_element_type=jnp.float32)
    onehot = ids[:, None] == jnp.arange(experts_all, dtype=jnp.int32)[None, :]
    gate = jax.nn.sigmoid(jnp.sum(jnp.where(onehot, logits, 0.0), axis=-1))
    grad_out = (gate[:, None] * cotangent[0].reshape(count_tok, width).astype(jnp.float32)).astype(
        jnp.bfloat16
    )
    running = jnp.cumsum(onehot.astype(jnp.int32), axis=0) - 1
    rank = jnp.sum(jnp.where(onehot, running, 0), axis=-1)
    slot = ids * cap + rank
    place = (slot[None, :] == jnp.arange(slots, dtype=jnp.int32)[:, None]).astype(jnp.bfloat16)
    send = jnp.dot(place, normed, preferred_element_type=jnp.float32).astype(jnp.bfloat16)
    send = send.reshape(n_sx, exp_dev, cap, width)
    send_grad = jnp.dot(place, grad_out, preferred_element_type=jnp.float32).astype(jnp.bfloat16)
    send_grad = send_grad.reshape(n_sx, exp_dev, cap, width)
    received = lax.all_to_all(send, "sx", split_axis=0, concat_axis=0, tiled=True)
    act = jnp.einsum("secd,edf->secf", received, w_up, preferred_element_type=jnp.float32)
    hidden = jax.nn.gelu(act).astype(jnp.bfloat16)
    expert_out = jnp.einsum(
        "secf,efd->secd", hidden, w_down, preferred_element_type=jnp.float32
    ).astype(jnp.bfloat16)
    returned = lax.all_to_all(expert_out, "sx", split_axis=0, concat_axis=0, tiled=True)
    moe = jnp.einsum(
        "st,sd->td", place, returned.reshape(slots, width), preferred_element_type=jnp.float32
    )
    mixed = (resid + gate[:, None] * moe).astype(jnp.bfloat16).reshape(1, rows_t, cols_t, width)
    received_grad = lax.all_to_all(send_grad, "sx", split_axis=0, concat_axis=0, tiled=True)
    full_up, full_down = expert_grads(received, received_grad, act, hidden, w_down)
    grad_up, grad_down = (
        lax.psum_scatter(
            full_up.astype(jnp.bfloat16), ("sy", "dp"), scatter_dimension=2, tiled=True
        ).astype(jnp.float32),
        lax.psum_scatter(
            full_down.astype(jnp.bfloat16), ("sy", "dp"), scatter_dimension=1, tiled=True
        ).astype(jnp.float32),
    )
    return (mixed, grad_up, grad_down)


def solution(mesh):
    return jax.shard_map(
        on_device,
        mesh=mesh,
        in_specs=(
            P("dp", "sy", "sx", None),
            P("dp", "sy", "sx", None),
            P(),
            P(),
            P(),
            P(),
            P("sx", None, None),
            P("sx", None, None),
            P("dp", "sy", "sx", None, None),
        ),
        out_specs=(
            P("dp", "sy", "sx", None),
            P("sx", None, ("sy", "dp")),
            P("sx", ("sy", "dp"), None),
        ),
        check_vma=False,
    )
```

profile of v0, /device:TPU:1, one launch (start us, length us, event | category | flops | bytes accessed | tf_op | source)
XLA Modules:
  0.0 367.9 jit_solution(10210683577001398583)
XLA Ops:
  7.2 0.0 copy-start
  7.2 1.1 slice_bitcast_fusion.5
  8.3 2.1 collective-permute-start
  10.4 0.1 add_bitcast_fusion.1
  10.5 0.1 eq.66
  10.6 1.7 copy.29
  12.3 4.3 %collective-permute-done = bf16[8,32,512]{2,1,0:T(8,128)(2,1)S(1)} collective-permute-done((bf16[8,32,512]{2,1,0:T(8,128)(2,1)S(1)}, bf16[8,32,512]{2,1,0:T(8,128)(2,1)S(1)}, u32[]{:S(2)}, u32[]{:S(2)}) %collective-permute-start) | collective-permute-done | bytes 262176 | tf_op jit(solution)/shard_map/ppermute | solution.py:13
  16.7 5.0 %collective-permute-start.1 = (bf16[16,8,512]{2,1,0:T(8,128)(2,1)S(1)}, bf16[16,8,512]{2,1,0:T(8,128)(2,1)S(1)}, u32[]{:S(2)}, u32[]{:S(2)}) collective-permute-start(bf16[16,8,512]{2,1,0:T(8,128)(2,1)S(1)} %pad_maximum_fusion.4), channel_id=1, source_target_pairs={{30,0},{0,2},{2,4},{4,6},{6,8},{8,10},{10,12},{12,14},{14,16},{16,... | collective-permute-start | bytes 393224 | tf_op jit(solution)/shard_map/ppermute | solution.py:13
  21.7 0.1 broadcast_compare_fusion
  21.8 1.8 collective-permute-done.1
  23.7 0.2 fusion.41
  23.9 0.3 fusion.44
  24.2 0.2 fusion.45
  24.5 1.0 fusion.71
  25.5 0.4 multiply_reduce_fusion.2
  25.9 8.6 %fusion.11 = (f32[2,16,256]{2,1,0:T(8,128)S(1)}, f32[2,16,256,256]{2,3,1,0:T(8,128)S(1)}) fusion(f32[16]{0:T(128)S(1)} %copy-done.6, pred[2,256,256]{1,2,0:T(8,128)(4,1)S(1)} %broadcast_compare_fusion, f32[2,256,3,16,32]{1,4,3,2,0:T(8,128)S(1)} %fusion.71, f32[2,256,16]{1,2,0:T(8,128)S(1)} %get-tuple-element.13, f32[2,256,16]{1,2,0:T(8,128)S(1)} %get-tuple-element.14), kind=kOutput, calls=%fused_computation.20 | convolution fusion | flops 812113920 | bytes 10715648 | tf_op jit(solution)/shard_map/wqhc,wkhc->whqk/dot_general | solution.py:36
  34.5 0.0 copy-start.3
  34.5 0.0 copy-start.2
  34.5 2.3 fusion.37
  36.8 0.5 copy.31
  37.4 0.0 copy-start.4
  37.4 0.1 copy.49
  37.5 0.0 copy-start.5
  37.5 0.5 convolution_convert_fusion
  38.0 3.7 %collective-permute-start.2 = (bf16[16,8,512]{2,1,0:T(8,128)(2,1)S(1)}, bf16[16,8,512]{2,1,0:T(8,128)(2,1)S(1)}, u32[]{:S(2)}, u32[]{:S(2)}) collective-permute-start(bf16[16,8,512]{2,1,0:T(8,128)(2,1)S(1)} %slice.65), channel_id=1, source_target_pairs={{2,0},{4,2},{6,4},{8,6},{10,8},{12,10},{14,12},{16,14},{18,16},{20... | collective-permute-start | bytes 393224 | tf_op jit(solution)/shard_map/ppermute | solution.py:13
  41.8 1.2 reduce-window.6
  42.9 0.2 slice_reduce_fusion
  43.2 0.0 collective-permute-done.2
  43.3 1.4 collective-permute-start.3
  44.7 0.1 fusion.65
  44.8 5.3 %collective-permute-done.3 = bf16[8,32,512]{2,1,0:T(8,128)(2,1)S(1)} collective-permute-done((bf16[8,32,512]{2,1,0:T(8,128)(2,1)S(1)}, bf16[8,32,512]{2,1,0:T(8,128)(2,1)S(1)}, u32[]{:S(2)}, u32[]{:S(2)}) %collective-permute-start.3) | collective-permute-done | bytes 262176 | tf_op jit(solution)/shard_map/ppermute | solution.py:13
  50.2 0.2 fusion.55
  50.4 0.1 div.54
  50.5 0.3 multiply_reduce_fusion
  50.8 0.1 rsqrt.22
  50.9 0.2 multiply_convert_fusion
  51.2 1.7 fusion.25
  52.9 9.4 %all-to-all-start = ((bf16[16,2,32,512]{3,2,1,0:T(8,128)(2,1)}), bf16[16,2,32,512]{3,2,1,0:T(8,128)(2,1)S(1)}, u32[]{:S(2)}, u32[]{:S(2)}) async-start(bf16[16,2,32,512]{3,2,1,0:T(8,128)(2,1)} %bitcast.181), calls=%async_computation | async-start | bytes 2097152 | tf_op jit(solution)/shard_map/all_to_all | solution.py:119
  62.3 0.3 fusion.38
  62.6 1.9 fusion.26
  64.4 25.8 %all-to-all-done = bf16[16,2,32,512]{3,2,1,0:T(8,128)(2,1)S(1)} async-done(((bf16[16,2,32,512]{3,2,1,0:T(8,128)(2,1)}), bf16[16,2,32,512]{3,2,1,0:T(8,128)(2,1)S(1)}, u32[]{:S(2)}, u32[]{:S(2)}) %all-to-all-start) | async-done | bytes 1048608 | tf_op jit(solution)/shard_map/all_to_all | solution.py:119
  90.2 4.2 %all-to-all-start.2 = ((bf16[16,2,32,512]{3,2,1,0:T(8,128)(2,1)}), bf16[16,2,32,512]{3,2,1,0:T(8,128)(2,1)}, u32[]{:S(2)}, u32[]{:S(2)}) async-start(bf16[16,2,32,512]{3,2,1,0:T(8,128)(2,1)} %bitcast.180), calls=%async_computation.2 | async-start | bytes 2097152 | tf_op jit(solution)/shard_map/all_to_all | solution.py:130
  94.4 0.0 reduce-scatter.7.cloned.1.call-start
  94.5 7.8 %fusion.12 = f32[2,16,32,2048]{3,2,1,0:T(8,128)} fusion(bf16[2,512,2048]{2,1,0:T(8,128)(2,1)} %param.15, bf16[16,2,32,512]{3,2,1,0:T(8,128)(2,1)S(1)} %all-to-all-done), kind=kOutput, calls=%fused_computation.21 | convolution fusion | flops 2147483648 | bytes 13631488 | tf_op jit(solution)/shard_map/secd,edf->secf/dot_general | solution.py:120
  102.2 19.5 %all-to-all-done.2 = bf16[16,2,32,512]{3,2,1,0:T(8,128)(2,1)} async-done(((bf16[16,2,32,512]{3,2,1,0:T(8,128)(2,1)}), bf16[16,2,32,512]{3,2,1,0:T(8,128)(2,1)}, u32[]{:S(2)}, u32[]{:S(2)}) %all-to-all-start.2) | async-done | bytes 1048608 | tf_op jit(solution)/shard_map/all_to_all | solution.py:130
  121.8 9.7 %fusion.6 = bf16[16,2,32,2048]{3,2,0,1:T(8,128)(2,1)S(1)} fusion(f32[2,16,32,2048]{3,2,1,0:T(8,128)} %fusion.12, bf16[2,2048,512]{2,1,0:T(8,128)(2,1)} %param.16, bf16[16,2,32,512]{3,2,1,0:T(8,128)(2,1)} %all-to-all-done.2), kind=kOutput, calls=%fused_computation.8 | convolution fusion | flops 2189426688 | bytes 17825792 | tf_op jit(solution)/shard_map/secd,efd->secf/dot_general | solution.py:51
  131.5 4.5 %bitcast_convert_fusion.1 = bf16[2,512,2048]{2,1,0:T(8,128)(2,1)} fusion(bf16[16,2,32,512]{3,2,1,0:T(8,128)(2,1)S(1)} %all-to-all-done, bf16[16,2,32,2048]{3,2,0,1:T(8,128)(2,1)S(1)} %fusion.6), kind=kOutput, calls=%fused_computation.10 | convolution fusion | flops 2149580800 | bytes 9437184 | tf_op jit(solution)/shard_map/secd,secf->edf/dot_general | solution.py:55
  135.9 11.2 %copy.46 = bf16[2,512,2048]{1,0,2:T(2,128)(2,1)} copy(bf16[2,512,2048]{2,1,0:T(8,128)(2,1)} %bitcast_convert_fusion.1) | data formatting | bytes 8388608
  147.1 5.4 %copy.50 = bf16[256,8,2,512]{3,1,2,0:T(8,128)(2,1)} copy(bf16[256,8,2,512]{3,2,1,0:T(2,128)(2,1)} %bitcast.167) | data formatting | bytes 8388608
  152.4 0.0 reduce-scatter.7.cloned.1.call-update
  152.4 0.3 reduce-scatter.5.cloned.1.call-start
  152.8 9.0 %bitcast_convert_fusion = bf16[2,2048,512]{2,1,0:T(8,128)(2,1)} fusion(bf16[16,2,32,512]{3,2,1,0:T(8,128)(2,1)} %all-to-all-done.2, f32[2,16,32,2048]{3,2,1,0:T(8,128)} %fusion.12), kind=kOutput, calls=%fused_computation.9 | convolution fusion | flops 2168455168 | bytes 13631488 | tf_op jit(solution)/shard_map/secf,secd->efd/dot_general | solution.py:48
  161.8 0.0 reduce-scatter.5.cloned.1.call-update
  161.8 0.0 copy-start.1
  161.8 7.4 %fusion.30 = bf16[16,2,32,512]{3,2,0,1:T(8,128)(2,1)S(1)} fusion(bf16[2,2048,512]{2,1,0:T(8,128)(2,1)} %param.16, f32[2,16,32,2048]{3,2,1,0:T(8,128)} %fusion.12), kind=kOutput, calls=%fused_computation.36 | convolution fusion | flops 2166882304 | bytes 13631488 | tf_op jit(solution)/shard_map/secf,efd->secd/dot_general | solution.py:122
  169.2 0.1 copy.35
  169.3 32.2 %all_to_all.15 = bf16[16,2,32,512]{3,2,1,0:T(8,128)(2,1)S(1)} all-to-all(bf16[16,2,32,512]{3,2,1,0:T(8,128)(2,1)S(1)} %copy.35), channel_id=1, replica_groups=mesh['sy'=8,'sx'=16,'dp'=2] {'sx'}, dimensions={0} | all-to-all | bytes 2097152 | tf_op jit(solution)/shard_map/all_to_all | solution.py:125
  201.5 1.6 fusion.36
  203.0 47.4 %reduce-scatter.7.cloned.1.call-done = bf16[128,1024]{1,0:T(8,128)(2,1)} async-done(((bf16[2048,1024]{1,0:T(8,128)(2,1)}), bf16[128,1024]{1,0:T(8,128)(2,1)}) %reduce-scatter.7.cloned.1.call-update) | async-done | bytes 262160
  250.4 1.1 reshape.256
  251.6 0.2 copy.47
  251.8 0.8 convert_element_type.154
  252.6 106.6 %reduce-scatter.5.cloned.1.call-done = bf16[2,128,512]{2,1,0:T(8,128)(2,1)} async-done(((bf16[2,2048,512]{2,1,0:T(8,128)(2,1)}), bf16[2,128,512]{2,1,0:T(8,128)(2,1)}) %reduce-scatter.5.cloned.1.call-update) | async-done | bytes 262160 | tf_op jit(solution)/shard_map/reduce_scatter | solution.py:136
  359.3 1.8 convert_element_type.156
  (28 shorter events, 0.4 us)
Async XLA Ops:
  7.2 30.3 %copy-start = (bf16[512,512]{1,0:T(8,128)(2,1)S(1)}, bf16[512,512]{1,0:T(8,128)(2,1)}, u32[]{:S(2)}) copy-start(bf16[512,512]{1,0:T(8,128)(2,1)} %param.12) | copy-start | bytes 1572868
  8.3 8.3 %collective-permute-start = (bf16[8,32,512]{2,1,0:T(8,128)(2,1)S(1)}, bf16[8,32,512]{2,1,0:T(8,128)(2,1)S(1)}, u32[]{:S(2)}, u32[]{:S(2)}) collective-permute-start(bf16[8,32,512]{2,1,0:T(8,128)(2,1)S(1)} %get-tuple-element.9), channel_id=1, source_target_pairs={{224,0},{0,32},{32,64},{64,96},{96,128},{128,160},{160,192},{192,2... | collective-permute-start | bytes 786440 | tf_op jit(solution)/shard_map/ppermute | solution.py:13
  10.6 15.3 %copy-start.6 = (f32[16]{0:T(128)S(1)}, f32[16]{0:T(128)}, u32[]{:S(2)}) copy-start(f32[16]{0:T(128)} %param.13) | copy-start | bytes 196
  16.7 7.0 %collective-permute-start.1 = (bf16[16,8,512]{2,1,0:T(8,128)(2,1)S(1)}, bf16[16,8,512]{2,1,0:T(8,128)(2,1)S(1)}, u32[]{:S(2)}, u32[]{:S(2)}) collective-permute-start(bf16[16,8,512]{2,1,0:T(8,128)(2,1)S(1)} %pad_maximum_fusion.4), channel_id=1, source_target_pairs={{30,0},{0,2},{2,4},{4,6},{6,8},{8,10},{10,12},{12,14},{14,16},{16,... | collective-permute-start | bytes 393224 | tf_op jit(solution)/shard_map/ppermute | solution.py:13
  34.5 7.2 %copy-start.3 = (s32[1,1,1,512,1]{3,4,2,1,0:T(1,128)S(1)}, s32[1,1,1,512,1]{3,4,2,1,0:T(1,128)}, u32[]{:S(2)}) copy-start(s32[1,1,1,512,1]{3,4,2,1,0:T(1,128)} %param.17) | copy-start | bytes 6148
  34.5 15.6 %copy-start.2 = (bf16[1,16,32,512]{3,2,1,0:T(8,128)(2,1)S(1)}, bf16[1,16,32,512]{3,2,1,0:T(8,128)(2,1)}, u32[]{:S(2)}) copy-start(bf16[1,16,32,512]{3,2,1,0:T(8,128)(2,1)} %param.9) | copy-start | bytes 1572868
  37.4 24.9 %copy-start.4 = (bf16[512,32]{0,1:T(8,128)(2,1)S(1)}, bf16[512,32]{0,1:T(8,128)(2,1)}, u32[]{:S(2)}) copy-start(bf16[512,32]{0,1:T(8,128)(2,1)} %param.14) | copy-start | bytes 98308
  37.5 25.1 %copy-start.5 = (bf16[1,16,32,512]{3,2,1,0:T(8,128)(2,1)S(1)}, bf16[1,16,32,512]{3,2,1,0:T(8,128)(2,1)}, u32[]{:S(2)}) copy-start(bf16[1,16,32,512]{3,2,1,0:T(8,128)(2,1)} %param.10) | copy-start | bytes 1572868
  38.0 5.2 %collective-permute-start.2 = (bf16[16,8,512]{2,1,0:T(8,128)(2,1)S(1)}, bf16[16,8,512]{2,1,0:T(8,128)(2,1)S(1)}, u32[]{:S(2)}, u32[]{:S(2)}) collective-permute-start(bf16[16,8,512]{2,1,0:T(8,128)(2,1)S(1)} %slice.65), channel_id=1, source_target_pairs={{2,0},{4,2},{6,4},{8,6},{10,8},{12,10},{14,12},{16,14},{18,16},{20... | collective-permute-start | bytes 393224 | tf_op jit(solution)/shard_map/ppermute | solution.py:13
  43.3 6.9 %collective-permute-start.3 = (bf16[8,32,512]{2,1,0:T(8,128)(2,1)S(1)}, bf16[8,32,512]{2,1,0:T(8,128)(2,1)S(1)}, u32[]{:S(2)}, u32[]{:S(2)}) collective-permute-start(bf16[8,32,512]{2,1,0:T(8,128)(2,1)S(1)} %get-tuple-element.8), channel_id=1, source_target_pairs={{32,0},{64,32},{96,64},{128,96},{160,128},{192,160},{224,192},{0,2... | collective-permute-start | bytes 786440 | tf_op jit(solution)/shard_map/ppermute | solution.py:13
  52.9 37.3 %all-to-all-start = ((bf16[16,2,32,512]{3,2,1,0:T(8,128)(2,1)}), bf16[16,2,32,512]{3,2,1,0:T(8,128)(2,1)S(1)}, u32[]{:S(2)}, u32[]{:S(2)}) async-start(bf16[16,2,32,512]{3,2,1,0:T(8,128)(2,1)} %bitcast.181), calls=%async_computation | async-start | bytes 2097152 | tf_op jit(solution)/shard_map/all_to_all | solution.py:119
  90.2 31.6 %all-to-all-start.2 = ((bf16[16,2,32,512]{3,2,1,0:T(8,128)(2,1)}), bf16[16,2,32,512]{3,2,1,0:T(8,128)(2,1)}, u32[]{:S(2)}, u32[]{:S(2)}) async-start(bf16[16,2,32,512]{3,2,1,0:T(8,128)(2,1)} %bitcast.180), calls=%async_computation.2 | async-start | bytes 2097152 | tf_op jit(solution)/shard_map/all_to_all | solution.py:130
  94.4 156.0 %reduce-scatter.7.cloned.1.call-start = ((), (), s32[]{:S(2)}) async-start(), calls=%async_computation.6 | async-start | bytes 4456448
  152.4 206.8 %reduce-scatter.5.cloned.1.call-start = ((), (), s32[]{:S(2)}) async-start(), calls=%async_computation.5 | async-start | bytes 4456448 | tf_op jit(solution)/shard_map/reduce_scatter | solution.py:136
  161.8 199.3 %copy-start.1 = (bf16[512,512]{1,0:T(8,128)(2,1)S(1)}, bf16[512,512]{1,0:T(8,128)(2,1)}, u32[]{:S(2)}) copy-start(bf16[512,512]{1,0:T(8,128)(2,1)} %param.12) | copy-start | bytes 1572868
Sparse Core Ops, SparseCore 0:
  152.6 97.8 reduce-scatter.6
  253.0 106.2 reduce-scatter.4
where the time goes:
time: 373 us; the launch traced here: 368 us
  waiting for transfers between devices  211 us (57%)
  matrix products  56.1 us (15%)
  blocking collectives  32.2 us (9%)
  starting transfers between devices  26.3 us (7%)
  local copies, waits for them, and re-layouts  22.1 us (6%)
  between operations  14.4 us (4%)
  other arithmetic  6.19 us (2%)
    reduce_scatter x1, waiting for transfers between devices, on_device(): lax.psum_scatter(full_down.astype(jnp.bfloat16), ('sy', 'dp'), scatter_di...  107 us
    unnamed x3, waiting for transfers between devices  47.4 us
    all_to_all x1, blocking collectives, on_device(): lax.all_to_all(expert_out, 'sx', split_axis=0, concat_axis=0, tiled=True)  32.2 us
    all_to_all x1, waiting for transfers between devices, on_device(): lax.all_to_all(send, 'sx', split_axis=0, concat_axis=0, tiled=True)  25.8 us
    unnamed x20, local copies, waits for them, and re-layouts  19.7 us
    all_to_all x1, waiting for transfers between devices, on_device(): lax.all_to_all(send_grad, 'sx', split_axis=0, concat_axis=0, tiled=True)  19.5 us
    ppermute x4, starting transfers between devices, from_behind(): return lax.ppermute(block, axis, route)  12.3 us
    ppermute x4, waiting for transfers between devices, from_behind(): return lax.ppermute(block, axis, route)  11.4 us
  transfers between devices with their start and end apart: 8, of which 7 were waited for; matrix products, arithmetic and copies ran while one was open for 9% of the time, Pallas kernels for 0%

commit v1 on v0

--- a/solution.py
+++ b/solution.py
@@ -1,10 +1,195 @@
 import jax
 import jax.numpy as jnp
 from jax import lax
+from jax.experimental import pallas as pl
+from jax.experimental.pallas import tpu as pltpu
 from jax.sharding import PartitionSpec as P
 
 WIN = 16
 SHIFT = 8
+MESH = pl.DeviceIdType.MESH
+BF16 = jnp.bfloat16
+F32 = jnp.float32
+
+
+class RingHalf:
+    def __init__(self, src, here_a, here_b, to_a, to_b, bufs1, bufs2, hold, out, sems):
+        self.src = src
+        self.pa, self.pb = here_a, here_b
+        self.to_a, self.to_b = to_a, to_b
+        self.bufs1, self.bufs2 = bufs1, bufs2
+        self.hold = hold
+        self.out = out
+        self.s1, self.r1, self.s2, self.r2 = sems
+        self.order = [lax.rem(here_b + d, 4) for d in (2, 1, 3, 0)]
+        self.sent = []
+
+    def copy1(self, ref, kind, way, k):
+        copy = pltpu.make_async_remote_copy(
+            src_ref=ref,
+            dst_ref=self.bufs1.at[kind, way, k],
+            send_sem=self.s1.at[kind, way, k],
+            recv_sem=self.r1.at[kind, way, k],
+            device_id=self.to_a[way],
+            device_id_type=MESH,
+        )
+        return copy
+
+    def copy2(self, ref, kind, way):
+        return pltpu.make_async_remote_copy(
+            src_ref=ref,
+            dst_ref=self.bufs2.at[kind, way],
+            send_sem=self.s2.at[kind, way],
+            recv_sem=self.r2.at[kind, way],
+            device_id=self.to_b[way],
+            device_id_type=MESH,
+        )
+
+    def start(self, copy):
+        copy.start()
+        self.sent.append(copy)
+
+    def ahead(self, way):
+        return lax.rem(self.pa + (1 if way == 0 else 3), 4)
+
+    def send_far(self, k):
+        for way in range(2):
+            ref = self.src(way, lax.rem(self.pa + 2, 4), self.order[k])
+            self.start(self.copy1(ref, 0, way, k))
+
+    def send_raw(self, k):
+        for way in range(2):
+            ref = self.src(1 - way, self.ahead(way), self.order[k])
+            self.start(self.copy1(ref, 1, way, k))
+
+    def pass_on(self, k):
+        for way in range(2):
+            got = self.bufs1.at[0, way, k]
+            mine = self.src(way, self.ahead(way), self.order[k])
+            self.copy1(mine, 0, way, k).wait_recv()
+            got[...] = (got[...].astype(F32) + mine[...].astype(F32)).astype(BF16)
+            self.start(self.copy1(got, 2, way, k))
+
+    def close1(self, k):
+        for e in range(2):
+            raw, acc = self.bufs1.at[1, 1 - e, k], self.bufs1.at[2, e, k]
+            mine = self.src(e, self.pa, self.order[k])
+            self.copy1(raw, 1, 1 - e, k).wait_recv()
+            self.copy1(acc, 2, e, k).wait_recv()
+            total = mine[...].astype(F32) + raw[...].astype(F32) + acc[...].astype(F32)
+            if k < 3:
+                self.hold[k, e] = total.astype(BF16)
+            else:
+                self.out[e] = total
+        if k == 0:
+            for way in range(2):
+                self.start(self.copy2(self.hold.at[0, way], 0, way))
+        elif k == 1:
+            self.start(self.copy2(self.hold.at[1, 1], 1, 0))
+        elif k == 2:
+            self.start(self.copy2(self.hold.at[2, 0], 1, 1))
+
+    def pass_on2(self):
+        for way in range(2):
+            got = self.bufs2.at[0, way]
+            self.copy2(got, 0, way).wait_recv()
+            got[...] = (got[...].astype(F32) + self.hold[1 + way, way].astype(F32)).astype(BF16)
+            self.start(self.copy2(got, 2, way))
+
+    def close2(self):
+        for e in range(2):
+            raw, acc = self.bufs2.at[1, 1 - e], self.bufs2.at[2, e]
+            self.copy2(raw, 1, 1 - e).wait_recv()
+            self.copy2(acc, 2, e).wait_recv()
+            self.out[e] = self.out[e] + raw[...].astype(F32) + acc[...].astype(F32)
+
+    def finish(self):
+        for copy in self.sent:
+            copy.wait_send()
+
+
+def ring_places():
+    sy, dp = lax.axis_index("sy"), lax.axis_index("dp")
+    y, x = sy // 2, dp * 2 + lax.rem(sy, 2)
+    to_x, to_y = [], []
+    for step in (1, 3):
+        nx, ny = lax.rem(x + step, 4), lax.rem(y + step, 4)
+        to_x.append({"sy": y * 2 + lax.rem(nx, 2), "dp": nx // 2})
+        to_y.append({"sy": ny * 2 + lax.rem(x, 2)})
+    return x, y, to_x, to_y
+
+
+def shard_of(x, y):
+    return y * 4 + lax.rem(x, 2) * 2 + x // 2
+
+
+def greet(targets):
+    barrier = pltpu.get_barrier_semaphore()
+    for target in targets:
+        pl.semaphore_signal(barrier, inc=1, device_id=target, device_id_type=MESH)
+    pl.semaphore_wait(barrier, len(targets))
+
+
+def reduce_kernel(up_ref, down_ref, oup_ref, odown_ref, u1, u2, uh, d1, d2, dh, *sems):
+    x, y, to_x, to_y = ring_places()
+    greet(to_x + to_y)
+
+    def up_src(e, ix, iy):
+        col = pl.multiple_of(shard_of(ix, iy) * 128, 128)
+        return up_ref.at[e, :, pl.ds(col, 128)]
+
+    def down_src(e, iy, ix):
+        row = pl.multiple_of(shard_of(ix, iy) * 128, 128)
+        return down_ref.at[e, pl.ds(row, 128), :]
+
+    halves = (
+        RingHalf(up_src, x, y, to_x, to_y, u1, u2, uh, oup_ref, sems[:4]),
+        RingHalf(down_src, y, x, to_y, to_x, d1, d2, dh, odown_ref, sems[4:]),
+    )
+    for k in range(4):
+        for half in halves:
+            half.send_far(k)
+    for k in range(4):
+        for half in halves:
+            half.send_raw(k)
+    for k in range(4):
+        for half in halves:
+            half.pass_on(k)
+    for k in range(4):
+        for half in halves:
+            half.close1(k)
+    for half in halves:
+        half.pass_on2()
+    for half in halves:
+        half.close2()
+    for half in halves:
+        half.finish()
+
+
+def reduce_grads(up, down):
+    dma = pltpu.SemaphoreType.DMA
+    return pl.pallas_call(
+        reduce_kernel,
+        out_shape=(
+            jax.ShapeDtypeStruct((2, 512, 128), F32),
+            jax.ShapeDtypeStruct((2, 128, 512), F32),
+        ),
+        in_specs=[pl.BlockSpec(memory_space=pltpu.VMEM)] * 2,
+        out_specs=(pl.BlockSpec(memory_space=pltpu.VMEM),) * 2,
+        scratch_shapes=[
+            pltpu.VMEM((3, 2, 4, 512, 128), BF16),
+            pltpu.VMEM((3, 2, 512, 128), BF16),
+            pltpu.VMEM((3, 2, 512, 128), BF16),
+            pltpu.VMEM((3, 2, 4, 128, 512), BF16),
+            pltpu.VMEM((3, 2, 128, 512), BF16),
+            pltpu.VMEM((3, 2, 128, 512), BF16),
+        ]
+        + [dma((3, 2, 4)), dma((3, 2, 4)), dma((3, 2)), dma((3, 2))] * 2,
+        compiler_params=pltpu.CompilerParams(
+            collective_id=0, has_side_effects=True, vmem_limit_bytes=48 * 1024 * 1024
+        ),
+        name="reduce_grads",
+    )(up, down)
 
 
 def from_behind(block, axis, distance):
@@ -83,39 +268,39 @@
         .transpose(0, 2, 1, 3)
         .reshape(rows_h * cols_w, length)
     )
-    attended = attend(windows, labels, w_qkv, w_proj, logit_scale)
-    attended = (
-        attended.reshape(rows_h, cols_w, WIN, WIN, width)
-        .transpose(0, 2, 1, 3, 4)
-        .reshape(rows_t, cols_t, width)
-    )
-    right = from_behind(attended[:, :SHIFT], "sx", -1)
-    col_home = jnp.concatenate([attended[:, SHIFT:], right], 1)
-    lower = from_behind(col_home[:SHIFT], "sy", -1)
-    attn_home = jnp.concatenate([col_home[SHIFT:], lower], 0)
     count_tok = rows_t * cols_t
-    resid = (tile.astype(jnp.float32) + attn_home.astype(jnp.float32)).reshape(count_tok, width)
-    normed = layer_norm(resid).astype(jnp.bfloat16)
     experts_all = w_router.shape[1]
     exp_dev = w_up.shape[0]
     n_sx = lax.axis_size("sx")
     cap = 2 * count_tok // experts_all
     slots = experts_all * cap
     ids = expert_ids.reshape(count_tok)
-    logits = jnp.dot(normed, w_router, preferred_element_type=jnp.float32)
     onehot = ids[:, None] == jnp.arange(experts_all, dtype=jnp.int32)[None, :]
-    gate = jax.nn.sigmoid(jnp.sum(jnp.where(onehot, logits, 0.0), axis=-1))
-    grad_out = (gate[:, None] * cotangent[0].reshape(count_tok, width).astype(jnp.float32)).astype(
-        jnp.bfloat16
-    )
     running = jnp.cumsum(onehot.astype(jnp.int32), axis=0) - 1
     rank = jnp.sum(jnp.where(onehot, running, 0), axis=-1)
     slot = ids * cap + rank
     place = (slot[None, :] == jnp.arange(slots, dtype=jnp.int32)[:, None]).astype(jnp.bfloat16)
+    send_cot = jnp.dot(
+        place, cotangent[0].reshape(count_tok, width), preferred_element_type=jnp.float32
+    ).astype(jnp.bfloat16)
+    send_cot = send_cot.reshape(n_sx, exp_dev, cap, width)
+    received_cot = lax.all_to_all(send_cot, "sx", split_axis=0, concat_axis=0, tiled=True)
+    attended = attend(windows, labels, w_qkv, w_proj, logit_scale)
+    attended = (
+        attended.reshape(rows_h, cols_w, WIN, WIN, width)
+        .transpose(0, 2, 1, 3, 4)
+        .reshape(rows_t, cols_t, width)
+    )
+    right = from_behind(attended[:, :SHIFT], "sx", -1)
+    col_home = jnp.concatenate([attended[:, SHIFT:], right], 1)
+    lower = from_behind(col_home[:SHIFT], "sy", -1)
+    attn_home = jnp.concatenate([col_home[SHIFT:], lower], 0)
+    resid = (tile.astype(jnp.float32) + attn_home.astype(jnp.float32)).reshape(count_tok, width)
+    normed = layer_norm(resid).astype(jnp.bfloat16)
+    logits = jnp.dot(normed, w_router, preferred_element_type=jnp.float32)
+    gate = jax.nn.sigmoid(jnp.sum(jnp.where(onehot, logits, 0.0), axis=-1))
     send = jnp.dot(place, normed, preferred_element_type=jnp.float32).astype(jnp.bfloat16)
     send = send.reshape(n_sx, exp_dev, cap, width)
-    send_grad = jnp.dot(place, grad_out, preferred_element_type=jnp.float32).astype(jnp.bfloat16)
-    send_grad = send_grad.reshape(n_sx, exp_dev, cap, width)
     received = lax.all_to_all(send, "sx", split_axis=0, concat_axis=0, tiled=True)
     act = jnp.einsum("secd,edf->secf", received, w_up, preferred_element_type=jnp.float32)
     hidden = jax.nn.gelu(act).astype(jnp.bfloat16)
@@ -127,16 +312,12 @@
         "st,sd->td", place, returned.reshape(slots, width), preferred_element_type=jnp.float32
     )
     mixed = (resid + gate[:, None] * moe).astype(jnp.bfloat16).reshape(1, rows_t, cols_t, width)
-    received_grad = lax.all_to_all(send_grad, "sx", split_axis=0, concat_axis=0, tiled=True)
+    routers = lax.dynamic_slice_in_dim(w_router, lax.axis_index("sx") * exp_dev, exp_dev, 1)
+    gates = jnp.einsum("secd,de->sec", received, routers, preferred_element_type=jnp.float32)
+    gates = jax.nn.sigmoid(gates)
+    received_grad = (gates[..., None] * received_cot.astype(jnp.float32)).astype(jnp.bfloat16)
     full_up, full_down = expert_grads(received, received_grad, act, hidden, w_down)
-    grad_up, grad_down = (
-        lax.psum_scatter(
-            full_up.astype(jnp.bfloat16), ("sy", "dp"), scatter_dimension=2, tiled=True
-        ).astype(jnp.float32),
-        lax.psum_scatter(
-            full_down.astype(jnp.bfloat16), ("sy", "dp"), scatter_dimension=1, tiled=True
-        ).astype(jnp.float32),
-    )
+    grad_up, grad_down = reduce_grads(full_up.astype(jnp.bfloat16), full_down.astype(jnp.bfloat16))
     return (mixed, grad_up, grad_down)
 
 

time: 373 us -> 196 us (0.53); the launches traced: 368 us -> 195 us
  waiting for transfers between devices: 211 us -> 54.8 us
  Pallas kernels: 0 us -> 51.4 us
  blocking collectives: 32.2 us -> 0 us
  local copies, waits for them, and re-layouts: 22.1 us -> 7.04 us
  between operations: 14.4 us -> 1.08 us
  matrix products: 56.1 us -> 46.8 us
  starting transfers between devices: 26.3 us -> 30.4 us
    reduce_scatter x1 -> x0, waiting for transfers between devices: 107 us -> none  [on_device(): lax.psum_scatter(full_down.astype(jnp.bfloat16), ('sy', 'dp'), scatter_di...]
    pallas_call x0 -> x1, Pallas kernels: none -> 51.4 us  [reduce_grads(): pl.pallas_call(reduce_kernel, out_shape=(jax.ShapeDtypeStruct((2, 512, 12...]
    unnamed x3 -> x0, waiting for transfers between devices: 47.4 us -> none
    all_to_all x1 -> x0, blocking collectives: 32.2 us -> none  [on_device(): lax.all_to_all(expert_out, 'sx', split_axis=0, concat_axis=0, tiled=True)]
    unnamed x20 -> x24, local copies, waits for them, and re-layouts: 19.7 us -> 3.69 us
    all_to_all x1 -> x2, starting transfers between devices: 4.23 us -> 8.69 us  [the longest x1 4.45 us: on_device(): lax.all_to_all(expert_out, 'sx', split_axis=0, concat_axis=0, tiled=True)]
    dot_general x1, matrix products: 7.4 us -> 2.97 us  [on_device(): jnp.einsum('secf,efd->secd', hidden, w_down, preferred_element_type=jnp.f...]
    all_to_all x1 -> x2, waiting for transfers between devices: 19.5 us -> 17.5 us  [the longest x1 17.5 us: on_device(): lax.all_to_all(send_cot, 'sx', split_axis=0, concat_axis=0, tiled=True)]
  transfers between devices with their start and end apart: 8 -> 7, of which waited for: 7 -> 5; matrix products, arithmetic and copies ran while one was open for 9% -> 18% of each run, Pallas kernels for 0% -> 26%
where the time goes in v1:
time: 196 us; the launch traced here: 195 us
  waiting for transfers between devices  54.8 us (28%)
  Pallas kernels  51.4 us (26%)
  matrix products  46.8 us (24%)
  starting transfers between devices  30.4 us (16%)
  local copies, waits for them, and re-layouts  7.04 us (4%)
  other arithmetic  3.59 us (2%)
    pallas_call x1, Pallas kernels, reduce_grads(): pl.pallas_call(reduce_kernel, out_shape=(jax.ShapeDtypeStruct((2, 512, 12...  51.4 us
    all_to_all x1, waiting for transfers between devices, on_device(): lax.all_to_all(send, 'sx', split_axis=0, concat_axis=0, tiled=True)  25.9 us
    all_to_all x1, waiting for transfers between devices, on_device(): lax.all_to_all(send_cot, 'sx', split_axis=0, concat_axis=0, tiled=True)  17.5 us
    ppermute x4, starting transfers between devices, from_behind(): return lax.ppermute(block, axis, route)  12.3 us
    ppermute x4, waiting for transfers between devices, from_behind(): return lax.ppermute(block, axis, route)  11.4 us
    dot_general x1, matrix products, expert_grads(): jnp.einsum('secd,efd->secf', rows_grad, w_down_part, preferred_element_ty...  10.7 us
    all_to_all x1, starting transfers between devices, on_device(): lax.all_to_all(send, 'sx', split_axis=0, concat_axis=0, tiled=True)  9.42 us
    dot_general x1, matrix products, attend(): jnp.einsum('wqhc,wkhc->whqk', query, keys, precision=lax.Precision.HIGHEST)  8.58 us
  transfers between devices with their start and end apart: 7, of which 5 were waited for; matrix products, arithmetic and copies ran while one was open for 18% of the time, Pallas kernels for 26%

profile of v1, /device:TPU:1, one launch (start us, length us, event | category | flops | bytes accessed | tf_op | source)
XLA Modules:
  0.0 195.2 jit_solution(13040189325300913463)
XLA Ops:
  0.6 0.0 copy-start
  0.6 1.1 slice_bitcast_fusion.5
  1.8 2.1 %collective-permute-start = (bf16[8,32,512]{2,1,0:T(8,128)(2,1)S(1)}, bf16[8,32,512]{2,1,0:T(8,128)(2,1)S(1)}, u32[]{:S(2)}, u32[]{:S(2)}) collective-permute-start(bf16[8,32,512]{2,1,0:T(8,128)(2,1)S(1)} %get-tuple-element.13), channel_id=1, source_target_pairs={{224,0},{0,32},{32,64},{64,96},{96,128},{128,160},{160,192},{192,2... | collective-permute-start | bytes 786440 | tf_op jit(solution)/shard_map/ppermute | solution.py:198
  3.9 0.1 add_bitcast_fusion.1
  4.0 0.1 eq.66
  4.1 1.7 copy.29
  5.8 4.3 %collective-permute-done = bf16[8,32,512]{2,1,0:T(8,128)(2,1)S(1)} collective-permute-done((bf16[8,32,512]{2,1,0:T(8,128)(2,1)S(1)}, bf16[8,32,512]{2,1,0:T(8,128)(2,1)S(1)}, u32[]{:S(2)}, u32[]{:S(2)}) %collective-permute-start) | collective-permute-done | bytes 262176 | tf_op jit(solution)/shard_map/ppermute | solution.py:198
  10.1 5.0 %collective-permute-start.1 = (bf16[16,8,512]{2,1,0:T(8,128)(2,1)S(1)}, bf16[16,8,512]{2,1,0:T(8,128)(2,1)S(1)}, u32[]{:S(2)}, u32[]{:S(2)}) collective-permute-start(bf16[16,8,512]{2,1,0:T(8,128)(2,1)S(1)} %pad_maximum_fusion.4), channel_id=1, source_target_pairs={{30,0},{0,2},{2,4},{4,6},{6,8},{8,10},{10,12},{12,14},{14,16},{16,... | collective-permute-start | bytes 393224 | tf_op jit(solution)/shard_map/ppermute | solution.py:198
  15.2 0.1 broadcast_compare_fusion
  15.3 1.8 collective-permute-done.1
  17.2 0.2 fusion.40
  17.3 0.3 fusion.43
  17.7 0.2 fusion.44
  18.0 1.0 fusion.75
  19.0 0.4 multiply_reduce_fusion.2
  19.4 0.0 copy-done.7
  19.4 8.6 %fusion.11 = (f32[2,16,256]{2,1,0:T(8,128)S(1)}, f32[2,16,256,256]{2,3,1,0:T(8,128)S(1)}) fusion(f32[16]{0:T(128)S(1)} %copy-done.7, pred[2,256,256]{1,2,0:T(8,128)(4,1)S(1)} %broadcast_compare_fusion, f32[2,256,3,16,32]{1,4,3,2,0:T(8,128)S(1)} %fusion.75, f32[2,256,16]{1,2,0:T(8,128)S(1)} %get-tuple-element.17, f32[2,256,16]{1,2,0:T(8,128)S(1)} %get-tuple-element.18), kind=kOutput, calls=%fused_computation.20 | convolution fusion | flops 812113920 | bytes 10715648 | tf_op jit(solution)/shard_map/wqhc,wkhc->whqk/dot_general | solution.py:221
  28.0 0.0 copy-start.6
  28.0 0.0 copy-start.4
  28.0 0.0 copy-start.2
  28.0 2.3 %fusion.37 = bf16[2,256,16,32]{1,3,2,0:T(8,128)(2,1)S(1)} fusion(f32[2,16,256,256]{2,3,1,0:T(8,128)S(1)} %get-tuple-element.16, f32[2,16,256]{2,1,0:T(8,128)S(1)} %get-tuple-element.15, f32[16]{0:T(128)S(1)} %copy-done.7, pred[2,256,256]{1,2,0:T(8,128)(4,1)S(1)} %broadcast_compare_fusion, f32[2,256,3,16,32]{1,4,3,2,0:T(8,128)S(1)} %fusion.75), kind=kOutput, calls=%fused_computation.43 | convolution fusion | flops 142868480 | bytes 9601536 | tf_op jit(solution)/shard_map/whqk,wkhc->wqhc/dot_general | solution.py:226
  30.3 0.5 copy.31
  30.8 0.0 copy-start.3
  30.8 0.1 copy.49
  30.9 0.5 convolution_convert_fusion
  31.5 3.7 %collective-permute-start.2 = (bf16[16,8,512]{2,1,0:T(8,128)(2,1)S(1)}, bf16[16,8,512]{2,1,0:T(8,128)(2,1)S(1)}, u32[]{:S(2)}, u32[]{:S(2)}) collective-permute-start(bf16[16,8,512]{2,1,0:T(8,128)(2,1)S(1)} %slice.65), channel_id=1, source_target_pairs={{2,0},{4,2},{6,4},{8,6},{10,8},{12,10},{14,12},{16,14},{18,16},{20... | collective-permute-start | bytes 393224 | tf_op jit(solution)/shard_map/ppermute | solution.py:198
  35.2 1.2 reduce-window.6
  36.4 0.2 slice_reduce_fusion
  36.7 0.0 collective-permute-done.2
  36.8 1.4 collective-permute-start.3
  38.2 0.1 fusion.64
  38.3 5.3 %collective-permute-done.3 = bf16[8,32,512]{2,1,0:T(8,128)(2,1)S(1)} collective-permute-done((bf16[8,32,512]{2,1,0:T(8,128)(2,1)S(1)}, bf16[8,32,512]{2,1,0:T(8,128)(2,1)S(1)}, u32[]{:S(2)}, u32[]{:S(2)}) %collective-permute-start.3) | collective-permute-done | bytes 262176 | tf_op jit(solution)/shard_map/ppermute | solution.py:198
  43.6 0.2 fusion.56
  43.8 0.1 div.60
  43.9 0.3 multiply_reduce_fusion
  44.2 0.1 rsqrt.22
  44.4 0.2 multiply_convert_fusion.1
  44.6 1.7 fusion.25
  46.3 9.4 %all-to-all-start = ((bf16[16,2,32,512]{3,2,1,0:T(8,128)(2,1)}), bf16[16,2,32,512]{3,2,1,0:T(8,128)(2,1)S(1)}, u32[]{:S(2)}, u32[]{:S(2)}) async-start(bf16[16,2,32,512]{3,2,1,0:T(8,128)(2,1)} %bitcast.191), calls=%async_computation | async-start | bytes 2097152 | tf_op jit(solution)/shard_map/all_to_all | solution.py:304
  55.7 0.0 copy-done
  55.8 1.7 fusion.26
  57.4 0.3 fusion.38
  57.7 25.9 %all-to-all-done = bf16[16,2,32,512]{3,2,1,0:T(8,128)(2,1)S(1)} async-done(((bf16[16,2,32,512]{3,2,1,0:T(8,128)(2,1)}), bf16[16,2,32,512]{3,2,1,0:T(8,128)(2,1)S(1)}, u32[]{:S(2)}, u32[]{:S(2)}) %all-to-all-start) | async-done | bytes 1048608 | tf_op jit(solution)/shard_map/all_to_all | solution.py:304
  83.6 4.2 %all-to-all-start.2 = ((bf16[16,2,32,512]{3,2,1,0:T(8,128)(2,1)}), bf16[16,2,32,512]{3,2,1,0:T(8,128)(2,1)}, u32[]{:S(2)}, u32[]{:S(2)}) async-start(bf16[16,2,32,512]{3,2,1,0:T(8,128)(2,1)} %bitcast.192), calls=%async_computation.2 | async-start | bytes 2097152 | tf_op jit(solution)/shard_map/all_to_all | solution.py:287
  87.9 0.0 copy-start.5
  87.9 4.7 %fusion.12 = f32[2,16,32,2048]{3,2,1,0:T(8,128)S(1)} fusion(bf16[2,512,2048]{2,1,0:T(8,128)(2,1)} %param.15, bf16[16,2,32,512]{3,2,1,0:T(8,128)(2,1)S(1)} %all-to-all-done), kind=kOutput, calls=%fused_computation.21 | convolution fusion | flops 2147483648 | bytes 13631488 | tf_op jit(solution)/shard_map/secd,edf->secf/dot_general | solution.py:305
  92.6 0.0 copy-done.5
  92.6 0.0 copy-start.1
  92.6 3.0 %fusion.30 = bf16[16,2,32,512]{3,2,0,1:T(8,128)(2,1)S(1)} fusion(bf16[2,2048,512]{2,1,0:T(8,128)(2,1)S(1)} %copy-done.5, f32[2,16,32,2048]{3,2,1,0:T(8,128)S(1)} %fusion.12), kind=kOutput, calls=%fused_computation.37 | convolution fusion | flops 2166882304 | bytes 13631488 | tf_op jit(solution)/shard_map/secf,efd->secd/dot_general | solution.py:307
  95.6 0.2 copy-done.1
  95.8 1.1 copy.35
  96.9 0.8 fusion.53
  97.7 17.5 %all-to-all-done.2 = bf16[16,2,32,512]{3,2,1,0:T(8,128)(2,1)} async-done(((bf16[16,2,32,512]{3,2,1,0:T(8,128)(2,1)}), bf16[16,2,32,512]{3,2,1,0:T(8,128)(2,1)}, u32[]{:S(2)}, u32[]{:S(2)}) %all-to-all-start.2) | async-done | bytes 1048608 | tf_op jit(solution)/shard_map/all_to_all | solution.py:287
  115.2 4.5 %all-to-all-start.1 = ((bf16[16,2,32,512]{3,2,1,0:T(8,128)(2,1)}), bf16[16,2,32,512]{3,2,1,0:T(8,128)(2,1)}, u32[]{:S(2)}, u32[]{:S(2)}) async-start(bf16[16,2,32,512]{3,2,1,0:T(8,128)(2,1)} %copy.35), calls=%async_computation.1 | async-start | bytes 2097152 | tf_op jit(solution)/shard_map/all_to_all | solution.py:310
  119.7 0.0 slice-start
  119.7 10.7 %fusion.6 = bf16[16,2,32,2048]{3,2,0,1:T(8,128)(2,1)S(1)} fusion(f32[2,16,32,2048]{3,2,1,0:T(8,128)} %copy-done.1, bf16[2,2048,512]{2,1,0:T(8,128)(2,1)} %param.16, bf16[16,2,32,512]{3,2,1,0:T(8,128)(2,1)} %all-to-all-done.2, f32[16,2,32]{2,1,0:T(2,128)S(1)} %fusion.69), kind=kOutput, calls=%fused_computation.8 | convolution fusion | flops 2190999552 | bytes 17829888 | tf_op jit(solution)/shard_map/secd,efd->secf/dot_general | solution.py:236
  130.4 0.0 slice-start.1
  130.4 2.4 %bitcast_convert_fusion.1.up_ref = bf16[2,512,2048]{2,1,0:T(8,128)(2,1)S(1)} fusion(bf16[16,2,32,512]{3,2,1,0:T(8,128)(2,1)S(1)} %all-to-all-done, bf16[16,2,32,2048]{3,2,0,1:T(8,128)(2,1)S(1)} %fusion.6), kind=kOutput, calls=%fused_computation.10 | convolution fusion | flops 2149580800 | bytes 9437184 | tf_op jit(solution)/shard_map/secd,secf->edf/dot_general | solution.py:240
  132.8 6.6 %bitcast_convert_fusion.down_ref = bf16[2,2048,512]{2,1,0:T(8,128)(2,1)} fusion(f32[2,16,32,2048]{3,2,1,0:T(8,128)S(1)} %bitcast.178, bf16[16,2,32,512]{3,2,1,0:T(8,128)(2,1)} %all-to-all-done.2, f32[16,2,32]{2,1,0:T(2,128)S(1)} %fusion.69), kind=kOutput, calls=%fused_computation.9 | convolution fusion | flops 2170028032 | bytes 13635584 | tf_op jit(solution)/shard_map/secf,secd->efd/dot_general | solution.py:233
  139.4 51.4 %reduce_grads.1 = (f32[2,512,128]{2,1,0:T(8,128)S(1)}, f32[2,128,512]{2,1,0:T(8,128)S(1)}) custom-call(bf16[2,512,2048]{2,1,0:T(8,128)(2,1)S(1)} %bitcast_convert_fusion.1.up_ref, bf16[2,2048,512]{2,1,0:T(8,128)(2,1)} %bitcast_convert_fusion.down_ref), custom_call_target="tpu_custom_call" | custom-call | tf_op jit(solution)/shard_map/reduce_grads/pallas_call | solution.py:171
  190.8 0.0 all-to-all-done.1
  190.8 2.8 %fusion.36 = bf16[512,512]{1,0:T(8,128)(2,1)} fusion(f32[512,512]{1,0:T(8,128)S(1)} %get-tuple-element.10, bf16[1024,512]{1,0:T(8,128)(2,1)} %bitcast.33, s32[512]{0:T(512)S(1)} %multiply_add_fusion, f32[512]{0:T(512)S(1)} %add_divide_fusion), kind=kOutput, calls=%fused_computation.42 | convolution fusion | flops 538181632 | bytes 2625536 | tf_op jit(solution)/shard_map/st,sd->td/dot_general | solution.py:311
  193.6 0.8 copy.66
  194.4 0.8 copy.67
  (30 shorter events, 0.5 us)
Async XLA Ops:
  0.6 55.1 %copy-start = (bf16[1,16,32,512]{3,2,1,0:T(8,128)(2,1)S(1)}, bf16[1,16,32,512]{3,2,1,0:T(8,128)(2,1)}, u32[]{:S(2)}) copy-start(bf16[1,16,32,512]{3,2,1,0:T(8,128)(2,1)} %param.10) | copy-start | bytes 1572868
  1.8 8.3 %collective-permute-start = (bf16[8,32,512]{2,1,0:T(8,128)(2,1)S(1)}, bf16[8,32,512]{2,1,0:T(8,128)(2,1)S(1)}, u32[]{:S(2)}, u32[]{:S(2)}) collective-permute-start(bf16[8,32,512]{2,1,0:T(8,128)(2,1)S(1)} %get-tuple-element.13), channel_id=1, source_target_pairs={{224,0},{0,32},{32,64},{64,96},{96,128},{128,160},{160,192},{192,2... | collective-permute-start | bytes 786440 | tf_op jit(solution)/shard_map/ppermute | solution.py:198
  4.1 15.3 %copy-start.7 = (f32[16]{0:T(128)S(1)}, f32[16]{0:T(128)}, u32[]{:S(2)}) copy-start(f32[16]{0:T(128)} %param.13) | copy-start | bytes 196
  10.1 7.0 %collective-permute-start.1 = (bf16[16,8,512]{2,1,0:T(8,128)(2,1)S(1)}, bf16[16,8,512]{2,1,0:T(8,128)(2,1)S(1)}, u32[]{:S(2)}, u32[]{:S(2)}) collective-permute-start(bf16[16,8,512]{2,1,0:T(8,128)(2,1)S(1)} %pad_maximum_fusion.4), channel_id=1, source_target_pairs={{30,0},{0,2},{2,4},{4,6},{6,8},{8,10},{10,12},{12,14},{14,16},{16,... | collective-permute-start | bytes 393224 | tf_op jit(solution)/shard_map/ppermute | solution.py:198
  28.0 3.0 %copy-start.6 = (bf16[512,512]{1,0:T(8,128)(2,1)S(1)}, bf16[512,512]{1,0:T(8,128)(2,1)}, u32[]{:S(2)}) copy-start(bf16[512,512]{1,0:T(8,128)(2,1)} %param.12) | copy-start | bytes 1572868
  28.0 7.2 %copy-start.4 = (s32[1,1,1,512,1]{3,4,2,1,0:T(1,128)S(1)}, s32[1,1,1,512,1]{3,4,2,1,0:T(1,128)}, u32[]{:S(2)}) copy-start(s32[1,1,1,512,1]{3,4,2,1,0:T(1,128)} %param.17) | copy-start | bytes 6148
  28.0 15.6 %copy-start.2 = (bf16[1,16,32,512]{3,2,1,0:T(8,128)(2,1)S(1)}, bf16[1,16,32,512]{3,2,1,0:T(8,128)(2,1)}, u32[]{:S(2)}) copy-start(bf16[1,16,32,512]{3,2,1,0:T(8,128)(2,1)} %param.9) | copy-start | bytes 1572868
  30.8 24.9 %copy-start.3 = (bf16[512,32]{0,1:T(8,128)(2,1)S(1)}, bf16[512,32]{0,1:T(8,128)(2,1)}, u32[]{:S(2)}) copy-start(bf16[512,32]{0,1:T(8,128)(2,1)} %param.14) | copy-start | bytes 98308
  31.5 5.2 %collective-permute-start.2 = (bf16[16,8,512]{2,1,0:T(8,128)(2,1)S(1)}, bf16[16,8,512]{2,1,0:T(8,128)(2,1)S(1)}, u32[]{:S(2)}, u32[]{:S(2)}) collective-permute-start(bf16[16,8,512]{2,1,0:T(8,128)(2,1)S(1)} %slice.65), channel_id=1, source_target_pairs={{2,0},{4,2},{6,4},{8,6},{10,8},{12,10},{14,12},{16,14},{18,16},{20... | collective-permute-start | bytes 393224 | tf_op jit(solution)/shard_map/ppermute | solution.py:198
  36.8 6.9 %collective-permute-start.3 = (bf16[8,32,512]{2,1,0:T(8,128)(2,1)S(1)}, bf16[8,32,512]{2,1,0:T(8,128)(2,1)S(1)}, u32[]{:S(2)}, u32[]{:S(2)}) collective-permute-start(bf16[8,32,512]{2,1,0:T(8,128)(2,1)S(1)} %get-tuple-element.12), channel_id=1, source_target_pairs={{32,0},{64,32},{96,64},{128,96},{160,128},{192,160},{224,192},{0,2... | collective-permute-start | bytes 786440 | tf_op jit(solution)/shard_map/ppermute | solution.py:198
  46.3 37.4 %all-to-all-start = ((bf16[16,2,32,512]{3,2,1,0:T(8,128)(2,1)}), bf16[16,2,32,512]{3,2,1,0:T(8,128)(2,1)S(1)}, u32[]{:S(2)}, u32[]{:S(2)}) async-start(bf16[16,2,32,512]{3,2,1,0:T(8,128)(2,1)} %bitcast.191), calls=%async_computation | async-start | bytes 2097152 | tf_op jit(solution)/shard_map/all_to_all | solution.py:304
  83.6 31.6 %all-to-all-start.2 = ((bf16[16,2,32,512]{3,2,1,0:T(8,128)(2,1)}), bf16[16,2,32,512]{3,2,1,0:T(8,128)(2,1)}, u32[]{:S(2)}, u32[]{:S(2)}) async-start(bf16[16,2,32,512]{3,2,1,0:T(8,128)(2,1)} %bitcast.192), calls=%async_computation.2 | async-start | bytes 2097152 | tf_op jit(solution)/shard_map/all_to_all | solution.py:287
  87.9 4.7 %copy-start.5 = (bf16[2,2048,512]{2,1,0:T(8,128)(2,1)S(1)}, bf16[2,2048,512]{2,1,0:T(8,128)(2,1)}, u32[]{:S(2)}) copy-start(bf16[2,2048,512]{2,1,0:T(8,128)(2,1)} %param.16) | copy-start | bytes 12582916
  92.6 3.2 %copy-start.1 = (f32[2,16,32,2048]{3,2,1,0:T(8,128)}, f32[2,16,32,2048]{3,2,1,0:T(8,128)S(1)}, u32[]{:S(2)}) copy-start(f32[2,16,32,2048]{3,2,1,0:T(8,128)S(1)} %fusion.12) | copy-start | bytes 25165828
  115.2 75.6 %all-to-all-start.1 = ((bf16[16,2,32,512]{3,2,1,0:T(8,128)(2,1)}), bf16[16,2,32,512]{3,2,1,0:T(8,128)(2,1)}, u32[]{:S(2)}, u32[]{:S(2)}) async-start(bf16[16,2,32,512]{3,2,1,0:T(8,128)(2,1)} %copy.35), calls=%async_computation.1 | async-start | bytes 2097152 | tf_op jit(solution)/shard_map/all_to_all | solution.py:310
  119.7 13.1 %slice-start = ((s8[8388608]{0:T(1024)(128)(4,1)}), s8[4194304]{0:T(1024)(128)(4,1)S(1)}, s32[]{:S(2)}) async-start(s8[8388608]{0:T(1024)(128)(4,1)} %bitcast.177), calls=%async_computation.3 | async-start | bytes 8388608
  130.4 2.4 %slice-start.1 = ((s8[8388608]{0:T(1024)(128)(4,1)}), s8[4194304]{0:T(1024)(128)(4,1)S(1)}, s32[]{:S(2)}) async-start(s8[8388608]{0:T(1024)(128)(4,1)} %bitcast.177), calls=%async_computation.4 | async-start | bytes 8388608

commit v2 on v0

v2 whole, which is shorter than its diff:
```python
import jax
import jax.numpy as jnp
from jax import lax
from jax.experimental import pallas as pl
from jax.experimental.pallas import tpu as pltpu
from jax.sharding import PartitionSpec as P

WIN = 16
SHIFT = 8
MESH = pl.DeviceIdType.MESH
BF16 = jnp.bfloat16
F32 = jnp.float32
N_SX = 16
CAP = 32
NEAR_FIRST = (0, 1, 15, 2, 14, 3, 13, 4, 12, 5, 11, 6, 10, 7, 9, 8)


def dot(a, b):
    return jnp.dot(a, b, preferred_element_type=F32)


def dot_tn(a, b):
    return lax.dot_general(a, b, (((0,), (0,)), ((), ())), preferred_element_type=F32)


def dot_nt(a, b):
    return lax.dot_general(a, b, (((1,), (1,)), ((), ())), preferred_element_type=F32)


def ring_places():
    sy, dp = lax.axis_index("sy"), lax.axis_index("dp")
    y, x = sy // 2, dp * 2 + lax.rem(sy, 2)
    to_x, to_y = [], []
    for step in (1, 3):
        nx, ny = lax.rem(x + step, 4), lax.rem(y + step, 4)
        to_x.append({"sy": y * 2 + lax.rem(nx, 2), "dp": nx // 2})
        to_y.append({"sy": ny * 2 + lax.rem(x, 2)})
    return x, y, to_x, to_y


def shard_of(x, y):
    return y * 4 + lax.rem(x, 2) * 2 + x // 2


def greet(targets):
    barrier = pltpu.get_barrier_semaphore()
    for target in targets:
        pl.semaphore_signal(barrier, inc=1, device_id=target, device_id_type=MESH)
    pl.semaphore_wait(barrier, len(targets))


class RingHalf:
    def __init__(self, block, here_a, here_b, to_a, to_b, stage, bufs1, bufs2, hold, out, sems):
        self.block = block
        self.pa, self.pb = here_a, here_b
        self.to_a, self.to_b = to_a, to_b
        self.stage, self.bufs1, self.bufs2 = stage, bufs1, bufs2
        self.hold = hold
        self.out = out
        self.s1, self.r1, self.s2, self.r2 = sems

    def order(self, k):
        return lax.rem(self.pb + 2 + k + (k // 2) * (1 + 2 * (k % 2)), 4)

    def copy1(self, kind, way, k):
        ref = self.bufs1.at[0, way, k] if kind == 2 else self.stage.at[kind, way, k]
        return pltpu.make_async_remote_copy(
            src_ref=ref,
            dst_ref=self.bufs1.at[kind, way, k],
            send_sem=self.s1.at[kind, way, k],
            recv_sem=self.r1.at[kind, way, k],
            device_id=self.to_a[way],
            device_id_type=MESH,
        )

    def copy2(self, kind, way):
        if kind == 0:
            ref = self.hold.at[0, way]
        elif kind == 1:
            ref = self.hold.at[1, 0] if way == 1 else self.hold.at[2, 1]
        else:
            ref = self.bufs2.at[0, way]
        return pltpu.make_async_remote_copy(
            src_ref=ref,
            dst_ref=self.bufs2.at[kind, way],
            send_sem=self.s2.at[kind, way],
            recv_sem=self.r2.at[kind, way],
            device_id=self.to_b[way],
            device_id_type=MESH,
        )

    def ahead(self, way):
        return lax.rem(self.pa + (1 if way == 0 else 3), 4)

    def send_far(self, k):
        for way in range(2):
            part = self.block(way, lax.rem(self.pa + 2, 4), self.order(k))
            self.stage[0, way, k] = part.astype(BF16)
            self.copy1(0, way, k).start()

    def send_raw(self, k):
        for way in range(2):
            part = self.block(1 - way, self.ahead(way), self.order(k))
            self.stage[1, way, k] = part.astype(BF16)
            self.copy1(1, way, k).start()

    def pass_on(self, k):
        for way in range(2):
            mine = self.block(way, self.ahead(way), self.order(k))
            self.copy1(0, way, k).wait_recv()
            self.bufs1[0, way, k] = (self.bufs1[0, way, k].astype(F32) + mine).astype(BF16)
            self.copy1(2, way, k).start()

    def close1(self, k):
        for e in range(2):
            total = self.block(e, self.pa, self.order(k))
            self.copy1(1, 1 - e, k).wait_recv()
            self.copy1(2, e, k).wait_recv()
            total = total + self.bufs1[1, 1 - e, k].astype(F32)
            total = total + self.bufs1[2, e, k].astype(F32)
            if k < 3:
                self.hold[k, e] = total.astype(BF16)
            else:
                self.out[e] = total
        if k == 0:
            self.copy2(0, 0).start()
            self.copy2(0, 1).start()
        elif k == 1:
            self.copy2(1, 1).start()
        elif k == 2:
            self.copy2(1, 0).start()

    def pass_on2(self):
        for way in range(2):
            self.copy2(0, way).wait_recv()
            mine = self.hold[2 - way, way].astype(F32)
            self.bufs2[0, way] = (self.bufs2[0, way].astype(F32) + mine).astype(BF16)
            self.copy2(2, way).start()

    def close2(self):
        for e in range(2):
            self.copy2(1, 1 - e).wait_recv()
            self.copy2(2, e).wait_recv()
            total = self.out[e] + self.bufs2[1, 1 - e].astype(F32)
            self.out[e] = total + self.bufs2[2, e].astype(F32)

    def finish(self):
        for kind in range(3):
            for way in range(2):
                for k in range(4):
                    self.copy1(kind, way, k).wait_send()
                self.copy2(kind, way).wait_send()


class Exchange:
    def __init__(self, me, away, source, landing, send_sem, recv_sem):
        self.me, self.away = me, away
        self.source, self.landing = source, landing
        self.send_sem, self.recv_sem = send_sem, recv_sem

    def peer(self, slot):
        d = NEAR_FIRST[slot]
        return lax.rem(self.me + (d if self.away else N_SX - d), N_SX)

    def copy(self, slot):
        peer = self.peer(slot)
        return pltpu.make_async_remote_copy(
            src_ref=self.source(slot, peer),
            dst_ref=self.landing(slot, self.me),
            send_sem=self.send_sem.at[slot],
            recv_sem=self.recv_sem.at[slot],
            device_id={"sx": peer},
            device_id_type=MESH,
        )


def gelu_parts(v):
    c = 0.7978845608028654
    sq = v * v
    t = jnp.tanh(c * v * (1.0 + 0.044715 * sq))
    half = 0.5 + 0.5 * t
    slope = half + (0.5 * c) * v * (1.0 - t * t) * (1.0 + (3 * 0.044715) * sq)
    return v * half, slope


def moe_kernel(
    send_ref, cot_ref, place_ref, resid_ref, gate_ref, router_ref, wup_any, wdown_any,
    mixed_ref, oup_ref, odown_ref,
    wup, wdown, recv, cotr, rgrad, rows_t, hidden, gact, rout, back,
    us, u1, u2, uh, ds, d1, d2, dh,
    wsem, lsem, xs, xr, cs, cr, bs, br, *sems,
):
    me = lax.axis_index("sx")
    x, y, to_x, to_y = ring_places()
    loads = []
    for e in range(2):
        loads.append(pltpu.make_async_copy(wup_any.at[e], wup.at[e], wsem.at[0, e]))
        loads.append(pltpu.make_async_copy(wdown_any.at[e], wdown.at[e], wsem.at[1, e]))
    for load in loads:
        load.start()
    rows_out = Exchange(
        me, True, lambda s, p: send_ref.at[p], lambda s, m: recv.at[:, s], xs, xr
    )
    cots_out = Exchange(
        me, True, lambda s, p: cot_ref.at[p], lambda s, m: cotr.at[:, s], cs, cr
    )
    home = Exchange(me, False, lambda s, p: rout.at[s], lambda s, m: back.at[m], bs, br)
    greet([{"sx": rows_out.peer(s)} for s in range(1, N_SX)] + to_x + to_y)
    for s in range(1, N_SX):
        rows_out.copy(s).start()
    for s in range(1, N_SX):
        cots_out.copy(s).start()
    recv[:, 0] = send_ref[me]
    cotr[:, 0] = cot_ref[me]
    for load in loads:
        load.wait()

    def hidden_part(g):
        for s in range(max(1, 8 * g), 8 * g + 8):
            rows_out.copy(s).wait_recv()
            cots_out.copy(s).wait_recv()
        for e in range(2):
            rows = recv[e, 8 * g : 8 * g + 8].reshape(256, 512)
            cot = cotr[e, 8 * g : 8 * g + 8].reshape(256, 512)
            logits = dot(rows, router_ref[...])
            column = lax.broadcasted_iota(jnp.int32, logits.shape, 1) == 2 * me + e
            gate = jax.nn.sigmoid(jnp.sum(jnp.where(column, logits, 0.0), axis=1, keepdims=True))
            grad = (gate * cot.astype(F32)).astype(BF16)
            rgrad[e, 256 * g : 256 * g + 256] = grad
            rows_t[e, :, 256 * g : 256 * g + 256] = rows.T

            def step(f, carry):
                part = pl.ds(pl.multiple_of(f * 512, 512), 512)
                act = dot(rows, wup[e, :, part])
                hid, slope = gelu_parts(act)
                hidden[e, 256 * g : 256 * g + 256, part] = hid.astype(BF16)
                through = dot_nt(grad, wdown[e, part, :])
                gact[e, 256 * g : 256 * g + 256, part] = (through * slope).astype(BF16)
                return carry

            lax.fori_loop(0, 4, step, 0)

    def return_part(g):
        for e in range(2):
            out = dot(hidden[e, 256 * g : 256 * g + 256], wdown[e]).astype(BF16)
            rout[8 * g : 8 * g + 8, e] = out.reshape(8, CAP, 512)
        for s in range(8 * g, 8 * g + 8):
            if s:
                home.copy(s).start()
        if g == 0:
            back[me] = rout[0]

    def up_block(e, ix, iy):
        col = pl.multiple_of(shard_of(ix, iy) * 128, 128)
        return dot(rows_t[e], gact[e, :, pl.ds(col, 128)])

    def down_block(e, iy, ix):
        col = pl.multiple_of(shard_of(ix, iy) * 128, 128)
        return dot_tn(hidden[e, :, pl.ds(col, 128)], rgrad[e])

    halves = (
        RingHalf(up_block, x, y, to_x, to_y, us, u1, u2, uh, oup_ref, sems[:4]),
        RingHalf(down_block, y, x, to_y, to_x, ds, d1, d2, dh, odown_ref, sems[4:]),
    )

    def each(method):
        def step(k, carry):
            for half in halves:
                getattr(half, method)(k)
            return carry

        lax.fori_loop(0, 4, step, 0)

    hidden_part(0)
    return_part(0)
    hidden_part(1)
    each("send_far")
    return_part(1)
    each("send_raw")
    each("pass_on")
    for k in range(4):
        for half in halves:
            half.close1(k)
    for half in halves:
        half.pass_on2()
    for s in range(1, N_SX):
        home.copy(s).wait_recv()
    moe = dot_tn(place_ref[...], back[...].reshape(1024, 512))
    mixed_ref[...] = (resid_ref[...] + gate_ref[...] * moe).astype(BF16)
    for half in halves:
        half.close2()
    for half in halves:
        half.finish()
    for s in range(1, N_SX):
        rows_out.copy(s).wait_send()
        cots_out.copy(s).wait_send()
        home.copy(s).wait_send()


def expert_layer(send, send_cot, place, resid, gate, w_router, w_up, w_down):
    dma = pltpu.SemaphoreType.DMA
    vmem = pl.BlockSpec(memory_space=pltpu.VMEM)
    anywhere = pl.BlockSpec(memory_space=pl.ANY)
    ring = [dma((3, 2, 4)), dma((3, 2, 4)), dma((3, 2)), dma((3, 2))]
    return pl.pallas_call(
        moe_kernel,
        out_shape=(
            jax.ShapeDtypeStruct((512, 512), BF16),
            jax.ShapeDtypeStruct((2, 512, 128), F32),
            jax.ShapeDtypeStruct((2, 128, 512), F32),
        ),
        in_specs=[vmem] * 6 + [anywhere] * 2,
        out_specs=(vmem,) * 3,
        scratch_shapes=[
            pltpu.VMEM((2, 512, 2048), BF16),
            pltpu.VMEM((2, 2048, 512), BF16),
            pltpu.VMEM((2, N_SX, CAP, 512), BF16),
            pltpu.VMEM((2, N_SX, CAP, 512), BF16),
            pltpu.VMEM((2, 512, 512), BF16),
            pltpu.VMEM((2, 512, 512), BF16),
            pltpu.VMEM((2, 512, 2048), BF16),
            pltpu.VMEM((2, 512, 2048), BF16),
            pltpu.VMEM((N_SX, 2, CAP, 512), BF16),
            pltpu.VMEM((N_SX, 2, CAP, 512), BF16),
            pltpu.VMEM((2, 2, 4, 512, 128), BF16),
            pltpu.VMEM((3, 2, 4, 512, 128), BF16),
            pltpu.VMEM((3, 2, 512, 128), BF16),
            pltpu.VMEM((3, 2, 512, 128), BF16),
            pltpu.VMEM((2, 2, 4, 128, 512), BF16),
            pltpu.VMEM((3, 2, 4, 128, 512), BF16),
            pltpu.VMEM((3, 2, 128, 512), BF16),
            pltpu.VMEM((3, 2, 128, 512), BF16),
            dma((2, 2)),
            dma((2,)),
        ]
        + [dma((N_SX,))] * 6
        + ring * 2,
        compiler_params=pltpu.CompilerParams(
            collective_id=0, has_side_effects=True, vmem_limit_bytes=56 * 1024 * 1024
        ),
        name="expert_layer",
    )(send, send_cot, place, resid, gate, w_router, w_up, w_down)


def from_behind(block, axis, distance):
    devices = range(lax.axis_size(axis))
    route = [((i - distance) % len(devices), i) for i in devices]
    return lax.ppermute(block, axis, route)


def layer_norm(values_in):
    mean = jnp.mean(values_in, axis=-1, keepdims=True)
    centred = values_in - mean
    return centred * lax.rsqrt(jnp.mean(centred * centred, axis=-1, keepdims=True) + 1e-05)


def attend(windows, labels, w_qkv, w_proj, logit_scale):
    count, length, width = windows.shape
    heads = logit_scale.shape[0]
    head_dim = width // heads
    normed = layer_norm(windows.astype(jnp.float32)).astype(jnp.bfloat16)
    mixed = jnp.dot(
        normed.reshape(count * length, width), w_qkv, preferred_element_type=jnp.float32
    )
    mixed = mixed.reshape(count, length, 3, heads, head_dim)
    query = mixed[:, :, 0]
    keys = mixed[:, :, 1]
    values = mixed[:, :, 2].astype(jnp.bfloat16)
    query = query / jnp.maximum(jnp.sqrt(jnp.sum(query * query, axis=-1, keepdims=True)), 4.0)
    keys = keys / jnp.maximum(jnp.sqrt(jnp.sum(keys * keys, axis=-1, keepdims=True)), 4.0)
    scores = jnp.einsum("wqhc,wkhc->whqk", query, keys, precision=lax.Precision.HIGHEST)
    scores = scores * logit_scale[None, :, None, None]
    allowed = labels[:, None, :, None] == labels[:, None, None, :]
    weights = jnp.where(allowed, jnp.exp(scores), 0.0)
    probs = (weights / jnp.sum(weights, axis=-1, keepdims=True)).astype(jnp.bfloat16)
    joined = jnp.einsum("whqk,wkhc->wqhc", probs, values, preferred_element_type=jnp.float32)
    joined = joined.astype(jnp.bfloat16).reshape(count * length, width)
    result = jnp.dot(joined, w_proj, preferred_element_type=jnp.float32).astype(jnp.bfloat16)
    return result.reshape(count, length, width)


def on_device(tokens, cotangent, w_qkv, w_proj, logit_scale, w_router, w_up, w_down, expert_ids):
    tile = tokens[0]
    rows_t, cols_t, width = tile.shape
    upper = from_behind(tile[rows_t - SHIFT :], "sy", 1)
    row_moved = jnp.concatenate([upper, tile[: rows_t - SHIFT]], 0)
    left = from_behind(row_moved[:, cols_t - SHIFT :], "sx", 1)
    region = jnp.concatenate([left, row_moved[:, : cols_t - SHIFT]], 1)
    row_label = jnp.where((lax.axis_index("sy") == 0) & (jnp.arange(rows_t) >= SHIFT), 1, 0).astype(
        jnp.int32
    )
    col_label = jnp.where((lax.axis_index("sx") == 0) & (jnp.arange(cols_t) >= SHIFT), 1, 0).astype(
        jnp.int32
    )
    label_map = row_label[:, None] * 2 + col_label[None, :]
    rows_h = rows_t // WIN
    cols_w = cols_t // WIN
    length = WIN * WIN
    windows = (
        region.reshape(rows_h, WIN, cols_w, WIN, width)
        .transpose(0, 2, 1, 3, 4)
        .reshape(rows_h * cols_w, length, width)
    )
    labels = (
        label_map.reshape(rows_h, WIN, cols_w, WIN)
        .transpose(0, 2, 1, 3)
        .reshape(rows_h * cols_w, length)
    )
    count_tok = rows_t * cols_t
    experts_all = w_router.shape[1]
    exp_dev = w_up.shape[0]
    n_sx = lax.axis_size("sx")
    cap = 2 * count_tok // experts_all
    slots = experts_all * cap
    ids = expert_ids.reshape(count_tok)
    onehot = ids[:, None] == jnp.arange(experts_all, dtype=jnp.int32)[None, :]
    running = jnp.cumsum(onehot.astype(jnp.int32), axis=0) - 1
    rank = jnp.sum(jnp.where(onehot, running, 0), axis=-1)
    slot = ids * cap + rank
    place = (slot[None, :] == jnp.arange(slots, dtype=jnp.int32)[:, None]).astype(jnp.bfloat16)
    send_cot = jnp.dot(
        place, cotangent[0].reshape(count_tok, width), preferred_element_type=jnp.float32
    ).astype(jnp.bfloat16)
    send_cot = send_cot.reshape(n_sx, exp_dev, cap, width)
    attended = attend(windows, labels, w_qkv, w_proj, logit_scale)
    attended = (
        attended.reshape(rows_h, cols_w, WIN, WIN, width)
        .transpose(0, 2, 1, 3, 4)
        .reshape(rows_t, cols_t, width)
    )
    right = from_behind(attended[:, :SHIFT], "sx", -1)
    col_home = jnp.concatenate([attended[:, SHIFT:], right], 1)
    lower = from_behind(col_home[:SHIFT], "sy", -1)
    attn_home = jnp.concatenate([col_home[SHIFT:], lower], 0)
    resid = (tile.astype(jnp.float32) + attn_home.astype(jnp.float32)).reshape(count_tok, width)
    normed = layer_norm(resid).astype(jnp.bfloat16)
    logits = jnp.dot(normed, w_router, preferred_element_type=jnp.float32)
    gate = jax.nn.sigmoid(jnp.sum(jnp.where(onehot, logits, 0.0), axis=-1))
    send = jnp.dot(place, normed, preferred_element_type=jnp.float32).astype(jnp.bfloat16)
    send = send.reshape(n_sx, exp_dev, cap, width)
    mixed, grad_up, grad_down = expert_layer(
        send, send_cot, place, resid, gate[:, None], w_router, w_up, w_down
    )
    mixed = mixed.reshape(1, rows_t, cols_t, width)
    return (mixed, grad_up, grad_down)


def solution(mesh):
    return jax.shard_map(
        on_device,
        mesh=mesh,
        in_specs=(
            P("dp", "sy", "sx", None),
            P("dp", "sy", "sx", None),
            P(),
            P(),
            P(),
            P(),
            P("sx", None, None),
            P("sx", None, None),
            P("dp", "sy", "sx", None, None),
        ),
        out_specs=(
            P("dp", "sy", "sx", None),
            P("sx", None, ("sy", "dp")),
            P("sx", ("sy", "dp"), None),
        ),
        check_vma=False,
    )
```

time: 373 us -> 167 us (0.45)
  waiting for transfers between devices: 211 us -> 6.04 us
  Pallas kernels: 0 us -> 110 us
  matrix products: 56.1 us -> 16 us
  blocking collectives: 32.2 us -> 0 us
  starting transfers between devices: 26.3 us -> 12.4 us
  between operations: 14.4 us -> 0.92 us
  local copies, waits for them, and re-layouts: 22.1 us -> 11.3 us
    pallas_call x0 -> x1, Pallas kernels: none -> 110 us  [expert_layer(): pl.pallas_call(moe_kernel, out_shape=(jax.ShapeDtypeStruct((512, 512), BF...]
    reduce_scatter x1 -> x0, waiting for transfers between devices: 107 us -> none  [on_device(): lax.psum_scatter(full_down.astype(jnp.bfloat16), ('sy', 'dp'), scatter_di...]
    unnamed x3 -> x0, waiting for transfers between devices: 47.4 us -> none
    all_to_all x2 -> x0, waiting for transfers between devices: 45.3 us -> none  [the longest x1 25.8 us: on_device(): lax.all_to_all(send, 'sx', split_axis=0, concat_axis=0, tiled=True)]
    dot_general x7 -> x1, matrix products: 41.7 us -> 1.69 us  [on_device(): jnp.dot(place, cotangent[0].reshape(count_tok, width), preferred_element_...]
    all_to_all x1 -> x0, blocking collectives: 32.2 us -> none  [on_device(): lax.all_to_all(expert_out, 'sx', split_axis=0, concat_axis=0, tiled=True)]
    all_to_all x2 -> x0, starting transfers between devices: 13.6 us -> none  [the longest x1 9.41 us: on_device(): lax.all_to_all(send, 'sx', split_axis=0, concat_axis=0, tiled=True)]
    unnamed x20 -> x18, local copies, waits for them, and re-layouts: 19.7 us -> 8.22 us
  transfers between devices with their start and end apart: 8 -> 4, of which waited for: 7 -> 3; matrix products, arithmetic and copies ran while one was open for 9% -> 5% of each run, Pallas kernels for 0% -> 0%
where the time goes in v2:
time: 167 us; the launch traced here: 164 us
  Pallas kernels  110 us (66%)
  matrix products  16 us (10%)
  starting transfers between devices  12.4 us (7%)
  local copies, waits for them, and re-layouts  11.3 us (7%)
  other arithmetic  7.31 us (4%)
  waiting for transfers between devices  6.04 us (4%)
    pallas_call x1, Pallas kernels, expert_layer(): pl.pallas_call(moe_kernel, out_shape=(jax.ShapeDtypeStruct((512, 512), BF...  110 us
    ppermute x4, starting transfers between devices, from_behind(): return lax.ppermute(block, axis, route)  12.4 us
    dot_general x1, matrix products, attend(): jnp.einsum('wqhc,wkhc->whqk', query, keys, precision=lax.Precision.HIGHEST)  8.57 us
    unnamed x18, local copies, waits for them, and re-layouts  8.22 us
    ppermute x4, waiting for transfers between devices, from_behind(): return lax.ppermute(block, axis, route)  6.04 us
  transfers between devices with their start and end apart: 4, of which 3 were waited for; matrix products, arithmetic and copies ran while one was open for 5% of the time, Pallas kernels for 0%

profile of v2, /device:TPU:1, one launch (start us, length us, event | category | flops | bytes accessed | tf_op | source)
XLA Modules:
  0.0 164.2 jit_solution(9813188986333548809)
XLA Ops:
  0.6 0.0 copy-start
  0.6 0.0 copy-start.3
  0.7 0.0 copy-start.2
  0.7 1.1 slice_bitcast_fusion.5
  1.8 2.1 %collective-permute-start = (bf16[8,32,512]{2,1,0:T(8,128)(2,1)S(1)}, bf16[8,32,512]{2,1,0:T(8,128)(2,1)S(1)}, u32[]{:S(2)}, u32[]{:S(2)}) collective-permute-start(bf16[8,32,512]{2,1,0:T(8,128)(2,1)S(1)} %get-tuple-element.15), channel_id=1, source_target_pairs={{224,0},{0,32},{32,64},{64,96},{96,128},{128,160},{160,192},{192,2... | collective-permute-start | bytes 786440 | tf_op jit(solution)/shard_map/ppermute | solution.py:348
  3.9 0.7 fusion.30
  4.6 1.2 reduce-window.6
  5.8 0.2 slice_reduce_fusion
  6.1 0.1 add_bitcast_fusion.1
  6.1 0.8 fusion.29
  6.9 1.7 %copy.20 = bf16[512,1536]{0,1:T(8,128)(2,1)S(1)} copy(bf16[512,1536]{1,0:T(8,128)(2,1)} %param.11) | data formatting | bytes 3145728 | tf_op args[2]
  8.6 0.1 eq.74
  8.7 0.0 copy-done.2
  8.7 0.8 copy.25.router_ref
  9.5 0.1 broadcast_compare_fusion
  9.6 0.5 collective-permute-done
  10.2 5.0 %collective-permute-start.1 = (bf16[16,8,512]{2,1,0:T(8,128)(2,1)S(1)}, bf16[16,8,512]{2,1,0:T(8,128)(2,1)S(1)}, u32[]{:S(2)}, u32[]{:S(2)}) collective-permute-start(bf16[16,8,512]{2,1,0:T(8,128)(2,1)S(1)} %pad_maximum_fusion.4), channel_id=1, source_target_pairs={{30,0},{0,2},{2,4},{4,6},{6,8},{8,10},{10,12},{12,14},{14,16},{16,... | collective-permute-start | bytes 393224 | tf_op jit(solution)/shard_map/ppermute | solution.py:348
  15.2 0.0 copy-done.3
  15.2 1.9 %collective-permute-done.1 = bf16[16,8,512]{2,1,0:T(8,128)(2,1)S(1)} collective-permute-done((bf16[16,8,512]{2,1,0:T(8,128)(2,1)S(1)}, bf16[16,8,512]{2,1,0:T(8,128)(2,1)S(1)}, u32[]{:S(2)}, u32[]{:S(2)}) %collective-permute-start.1) | collective-permute-done | bytes 131104 | tf_op jit(solution)/shard_map/ppermute | solution.py:348
  17.2 0.2 fusion.11
  17.4 0.3 fusion.14
  17.7 0.2 fusion.15
  18.0 0.0 copy-start.5
  18.0 1.0 fusion.33
  19.0 0.4 multiply_reduce_fusion.2
  19.4 0.0 copy-done.5
  19.4 8.6 %fusion = (f32[2,16,256]{2,1,0:T(8,128)S(1)}, f32[2,16,256,256]{2,3,1,0:T(8,128)S(1)}) fusion(f32[16]{0:T(128)S(1)} %copy-done.5, pred[2,256,256]{1,2,0:T(8,128)(4,1)S(1)} %broadcast_compare_fusion, f32[2,256,3,16,32]{1,4,3,2,0:T(8,128)S(1)} %fusion.33, f32[2,256,16]{1,2,0:T(8,128)S(1)} %get-tuple-element.19, f32[2,256,16]{1,2,0:T(8,128)S(1)} %get-tuple-element.20), kind=kOutput, calls=%fused_computation.2 | convolution fusion | flops 812113920 | bytes 10715648 | tf_op jit(solution)/shard_map/wqhc,wkhc->whqk/dot_general | solution.py:371
  28.0 0.0 copy-start.4
  28.0 2.3 %fusion.8 = bf16[2,256,16,32]{1,3,2,0:T(8,128)(2,1)S(1)} fusion(f32[2,16,256,256]{2,3,1,0:T(8,128)S(1)} %get-tuple-element.18, f32[2,16,256]{2,1,0:T(8,128)S(1)} %get-tuple-element.17, f32[16]{0:T(128)S(1)} %copy-done.5, pred[2,256,256]{1,2,0:T(8,128)(4,1)S(1)} %broadcast_compare_fusion, f32[2,256,3,16,32]{1,4,3,2,0:T(8,128)S(1)} %fusion.33), kind=kOutput, calls=%fused_computation.12 | convolution fusion | flops 142868480 | bytes 9601536 | tf_op jit(solution)/shard_map/whqk,wkhc->wqhc/dot_general | solution.py:376
  30.3 0.5 copy.22
  30.8 0.1 copy.29
  30.9 0.0 copy-done.4
  30.9 0.5 convolution_convert_fusion
  31.5 0.0 copy-start.1
  31.5 3.7 %collective-permute-start.2 = (bf16[16,8,512]{2,1,0:T(8,128)(2,1)S(1)}, bf16[16,8,512]{2,1,0:T(8,128)(2,1)S(1)}, u32[]{:S(2)}, u32[]{:S(2)}) collective-permute-start(bf16[16,8,512]{2,1,0:T(8,128)(2,1)S(1)} %slice.66), channel_id=1, source_target_pairs={{2,0},{4,2},{6,4},{8,6},{10,8},{12,10},{14,12},{16,14},{18,16},{20... | collective-permute-start | bytes 393224 | tf_op jit(solution)/shard_map/ppermute | solution.py:348
  35.2 1.4 fusion.2.place_ref
  36.6 0.0 collective-permute-done.2
  36.7 1.5 collective-permute-start.3
  38.2 0.0 copy-done
  38.2 1.7 %fusion.6 = bf16[1024,512]{1,0:T(8,128)(2,1)} fusion(bf16[512,512]{1,0:T(8,128)(2,1)S(1)} %bitcast.107, s32[512]{0:T(512)S(1)} %multiply_add_fusion), kind=kOutput, calls=%fused_computation.9 | convolution fusion | flops 537919488 | bytes 1574912 | tf_op jit(solution)/shard_map/dot_general | solution.py:421
  39.9 3.6 %collective-permute-done.3 = bf16[8,32,512]{2,1,0:T(8,128)(2,1)S(1)} collective-permute-done((bf16[8,32,512]{2,1,0:T(8,128)(2,1)S(1)}, bf16[8,32,512]{2,1,0:T(8,128)(2,1)S(1)}, u32[]{:S(2)}, u32[]{:S(2)}) %collective-permute-start.3) | collective-permute-done | bytes 262176 | tf_op jit(solution)/shard_map/ppermute | solution.py:348
  43.5 0.0 copy-done.1
  43.5 0.2 fusion.21
  43.7 0.3 multiply_reduce_fusion
  44.0 0.1 div.60
  44.1 0.1 rsqrt.22
  44.3 1.2 convert_add_fusion
  45.5 1.7 %fusion.5 = bf16[1024,512]{1,0:T(8,128)(2,1)} fusion(bf16[512,512]{1,0:T(8,128)(2,1)S(1)} %get-tuple-element.12, s32[512]{0:T(512)S(1)} %multiply_add_fusion), kind=kOutput, calls=%fused_computation.8 | convolution fusion | flops 537919488 | bytes 1574912 | tf_op jit(solution)/shard_map/dot_general | solution.py:439
  47.2 0.3 fusion.9
  47.5 0.9 copy.24.gate_ref
  48.4 110.2 %expert_layer.1 = (bf16[512,512]{1,0:T(8,128)(2,1)}, f32[2,512,128]{2,1,0:T(8,128)}, f32[2,128,512]{2,1,0:T(8,128)}) custom-call(bf16[16,2,32,512]{3,2,1,0:T(8,128)(2,1)} %bitcast.121, bf16[16,2,32,512]{3,2,1,0:T(8,128)(2,1)} %bitcast.120, bf16[1024,512]{1,0:T(8,128)(2,1)} %fusion.2.place_ref, f32[512,512]{1,0:T(8,128)} %get-tuple-element.11.resid_ref, ...), custom_call_target="tpu_custom_call" | custom-call | tf_op jit(solution)/shard_map/expert_layer/pallas_call | solution.py:305
  158.5 1.9 %copy.34 = bf16[1,16,32,512]{3,2,1,0:T(8,128)(2,1)} copy(bf16[1,16,32,512]{3,2,1,0:T(8,128)(2,1)} %bitcast.122) | data formatting | bytes 1048576
  160.4 1.9 %copy.35 = f32[2,512,128]{2,1,0:T(8,128)} copy(f32[2,512,128]{2,1,0:T(8,128)} %get-tuple-element.25) | data formatting | bytes 1048576
  162.3 1.9 %copy.36 = f32[2,128,512]{2,1,0:T(8,128)} copy(f32[2,128,512]{2,1,0:T(8,128)} %get-tuple-element.26) | data formatting | bytes 1048576
  (19 shorter events, 0.4 us)
Async XLA Ops:
  0.6 37.6 %copy-start = (bf16[1,16,32,512]{3,2,1,0:T(8,128)(2,1)S(1)}, bf16[1,16,32,512]{3,2,1,0:T(8,128)(2,1)}, u32[]{:S(2)}) copy-start(bf16[1,16,32,512]{3,2,1,0:T(8,128)(2,1)} %param.10) | copy-start | bytes 1572868
  0.6 14.5 %copy-start.3 = (s32[1,1,1,512,1]{3,4,2,1,0:T(1,128)S(1)}, s32[1,1,1,512,1]{3,4,2,1,0:T(1,128)}, u32[]{:S(2)}) copy-start(s32[1,1,1,512,1]{3,4,2,1,0:T(1,128)} %param.17) | copy-start | bytes 6148
  0.7 8.1 %copy-start.2 = (bf16[512,32]{0,1:T(8,128)(2,1)S(1)}, bf16[512,32]{0,1:T(8,128)(2,1)}, u32[]{:S(2)}) copy-start(bf16[512,32]{0,1:T(8,128)(2,1)} %param.14) | copy-start | bytes 98308
  1.8 8.3 %collective-permute-start = (bf16[8,32,512]{2,1,0:T(8,128)(2,1)S(1)}, bf16[8,32,512]{2,1,0:T(8,128)(2,1)S(1)}, u32[]{:S(2)}, u32[]{:S(2)}) collective-permute-start(bf16[8,32,512]{2,1,0:T(8,128)(2,1)S(1)} %get-tuple-element.15), channel_id=1, source_target_pairs={{224,0},{0,32},{32,64},{64,96},{96,128},{128,160},{160,192},{192,2... | collective-permute-start | bytes 786440 | tf_op jit(solution)/shard_map/ppermute | solution.py:348
  10.2 7.0 %collective-permute-start.1 = (bf16[16,8,512]{2,1,0:T(8,128)(2,1)S(1)}, bf16[16,8,512]{2,1,0:T(8,128)(2,1)S(1)}, u32[]{:S(2)}, u32[]{:S(2)}) collective-permute-start(bf16[16,8,512]{2,1,0:T(8,128)(2,1)S(1)} %pad_maximum_fusion.4), channel_id=1, source_target_pairs={{30,0},{0,2},{2,4},{4,6},{6,8},{8,10},{10,12},{12,14},{14,16},{16,... | collective-permute-start | bytes 393224 | tf_op jit(solution)/shard_map/ppermute | solution.py:348
  18.0 1.4 copy-start.5
  28.0 2.9 %copy-start.4 = (bf16[512,512]{1,0:T(8,128)(2,1)S(1)}, bf16[512,512]{1,0:T(8,128)(2,1)}, u32[]{:S(2)}) copy-start(bf16[512,512]{1,0:T(8,128)(2,1)} %param.12) | copy-start | bytes 1572868
  31.5 12.0 %copy-start.1 = (bf16[1,16,32,512]{3,2,1,0:T(8,128)(2,1)S(1)}, bf16[1,16,32,512]{3,2,1,0:T(8,128)(2,1)}, u32[]{:S(2)}) copy-start(bf16[1,16,32,512]{3,2,1,0:T(8,128)(2,1)} %param.9) | copy-start | bytes 1572868
  31.5 5.2 %collective-permute-start.2 = (bf16[16,8,512]{2,1,0:T(8,128)(2,1)S(1)}, bf16[16,8,512]{2,1,0:T(8,128)(2,1)S(1)}, u32[]{:S(2)}, u32[]{:S(2)}) collective-permute-start(bf16[16,8,512]{2,1,0:T(8,128)(2,1)S(1)} %slice.66), channel_id=1, source_target_pairs={{2,0},{4,2},{6,4},{8,6},{10,8},{12,10},{14,12},{16,14},{18,16},{20... | collective-permute-start | bytes 393224 | tf_op jit(solution)/shard_map/ppermute | solution.py:348
  36.7 6.8 %collective-permute-start.3 = (bf16[8,32,512]{2,1,0:T(8,128)(2,1)S(1)}, bf16[8,32,512]{2,1,0:T(8,128)(2,1)S(1)}, u32[]{:S(2)}, u32[]{:S(2)}) collective-permute-start(bf16[8,32,512]{2,1,0:T(8,128)(2,1)S(1)} %get-tuple-element.14), channel_id=1, source_target_pairs={{32,0},{64,32},{96,64},{128,96},{160,128},{192,160},{224,192},{0,2... | collective-permute-start | bytes 786440 | tf_op jit(solution)/shard_map/ppermute | solution.py:348

commit v3 on v2

v3 whole, which is shorter than its diff:
```python
import jax
import jax.numpy as jnp
from jax import lax
from jax.experimental import pallas as pl
from jax.experimental.pallas import tpu as pltpu
from jax.sharding import PartitionSpec as P

MESH = pl.DeviceIdType.MESH
BF16 = jnp.bfloat16
F32 = jnp.float32
N_SX = 16
VMEM_MIB = 52
CAP = 32
NEAR_FIRST = (0, 1, 15, 2, 14, 3, 13, 4, 12, 5, 11, 6, 10, 7, 9, 8)


def dot(a, b):
    return jnp.dot(a, b, preferred_element_type=F32)


def dot_tn(a, b):
    return lax.dot_general(a, b, (((0,), (0,)), ((), ())), preferred_element_type=F32)


def dot_nt(a, b):
    return lax.dot_general(a, b, (((1,), (1,)), ((), ())), preferred_element_type=F32)


def ring_places():
    sy, dp = lax.axis_index("sy"), lax.axis_index("dp")
    y, x = sy // 2, dp * 2 + lax.rem(sy, 2)
    to_x, to_y = [], []
    for step in (1, 3):
        nx, ny = lax.rem(x + step, 4), lax.rem(y + step, 4)
        to_x.append({"sy": y * 2 + lax.rem(nx, 2), "dp": nx // 2})
        to_y.append({"sy": ny * 2 + lax.rem(x, 2)})
    return x, y, to_x, to_y


def shard_of(x, y):
    return y * 4 + lax.rem(x, 2) * 2 + x // 2


class RingHalf:
    def __init__(self, block, here_a, here_b, to_a, to_b, stage, bufs1, bufs2, hold, out, sems):
        self.block = block
        self.pa, self.pb = here_a, here_b
        self.to_a, self.to_b = to_a, to_b
        self.stage, self.bufs1, self.bufs2 = stage, bufs1, bufs2
        self.hold = hold
        self.out = out
        self.s1, self.r1, self.s2, self.r2 = sems

    def order(self, k):
        return lax.rem(self.pb + 2 + k + (k // 2) * (1 + 2 * (k % 2)), 4)

    def copy1(self, kind, way, k):
        ref = self.bufs1.at[0, way, k] if kind == 2 else self.stage.at[kind, way, k]
        return pltpu.make_async_remote_copy(
            src_ref=ref,
            dst_ref=self.bufs1.at[kind, way, k],
            send_sem=self.s1.at[kind, way, k],
            recv_sem=self.r1.at[kind, way, k],
            device_id=self.to_a[way],
            device_id_type=MESH,
        )

    def copy2(self, kind, way):
        if kind == 0:
            ref = self.hold.at[0, way]
        elif kind == 1:
            ref = self.hold.at[1, 0] if way == 1 else self.hold.at[2, 1]
        else:
            ref = self.bufs2.at[0, way]
        return pltpu.make_async_remote_copy(
            src_ref=ref,
            dst_ref=self.bufs2.at[kind, way],
            send_sem=self.s2.at[kind, way],
            recv_sem=self.r2.at[kind, way],
            device_id=self.to_b[way],
            device_id_type=MESH,
        )

    def ahead(self, way):
        return lax.rem(self.pa + (1 if way == 0 else 3), 4)

    def send_far(self, k):
        for way in range(2):
            part = self.block(way, lax.rem(self.pa + 2, 4), self.order(k))
            self.stage[0, way, k] = part.astype(BF16)
            self.copy1(0, way, k).start()

    def send_raw(self, k):
        for way in range(2):
            part = self.block(1 - way, self.ahead(way), self.order(k))
            self.stage[1, way, k] = part.astype(BF16)
            self.copy1(1, way, k).start()

    def pass_on(self, k):
        for way in range(2):
            mine = self.block(way, self.ahead(way), self.order(k))
            self.copy1(0, way, k).wait_recv()
            self.bufs1[0, way, k] = (self.bufs1[0, way, k].astype(F32) + mine).astype(BF16)
            self.copy1(2, way, k).start()

    def close1(self, k):
        for e in range(2):
            total = self.block(e, self.pa, self.order(k))
            self.copy1(1, 1 - e, k).wait_recv()
            self.copy1(2, e, k).wait_recv()
            total = total + self.bufs1[1, 1 - e, k].astype(F32)
            total = total + self.bufs1[2, e, k].astype(F32)
            if k < 3:
                self.hold[k, e] = total.astype(BF16)
            else:
                self.out[e] = total
        if k == 0:
            self.copy2(0, 0).start()
            self.copy2(0, 1).start()
        elif k == 1:
            self.copy2(1, 1).start()
        elif k == 2:
            self.copy2(1, 0).start()

    def pass_on2(self):
        for way in range(2):
            self.copy2(0, way).wait_recv()
            mine = self.hold[2 - way, way].astype(F32)
            self.bufs2[0, way] = (self.bufs2[0, way].astype(F32) + mine).astype(BF16)
            self.copy2(2, way).start()

    def close2(self):
        for e in range(2):
            self.copy2(1, 1 - e).wait_recv()
            self.copy2(2, e).wait_recv()
            total = self.out[e] + self.bufs2[1, 1 - e].astype(F32)
            self.out[e] = total + self.bufs2[2, e].astype(F32)

    def finish(self):
        for kind in range(3):
            for way in range(2):
                for k in range(4):
                    self.copy1(kind, way, k).wait_send()
                self.copy2(kind, way).wait_send()


class Exchange:
    def __init__(self, me, away, source, landing, send_sem, recv_sem):
        self.me, self.away = me, away
        self.source, self.landing = source, landing
        self.send_sem, self.recv_sem = send_sem, recv_sem

    def peer(self, slot):
        d = NEAR_FIRST[slot]
        return lax.rem(self.me + (d if self.away else N_SX - d), N_SX)

    def copy(self, slot):
        peer = self.peer(slot)
        return pltpu.make_async_remote_copy(
            src_ref=self.source(slot, peer),
            dst_ref=self.landing(slot, self.me),
            send_sem=self.send_sem.at[slot],
            recv_sem=self.recv_sem.at[slot],
            device_id={"sx": peer},
            device_id_type=MESH,
        )


def gelu_parts(v):
    c = 0.7978845608028654
    sq = v * v
    t = jnp.tanh(c * v * (1.0 + 0.044715 * sq))
    half = 0.5 + 0.5 * t
    slope = half + (0.5 * c) * v * (1.0 - t * t) * (1.0 + (3 * 0.044715) * sq)
    return v * half, slope


def layer_norm(v):
    centred = v - jnp.mean(v, axis=-1, keepdims=True)
    return centred * lax.rsqrt(jnp.mean(centred * centred, axis=-1, keepdims=True) + 1e-05)


def split(v):
    high = v.astype(BF16)
    return high, (v - high.astype(F32)).astype(BF16)


def head_inverse(v, ones):
    high, low = split(v * v)
    total = dot(jnp.concatenate([high, low], axis=1), ones)
    return jnp.minimum(lax.rsqrt(total), 0.25)


def attend_group(qkv, joined, g, scale_ref, ones, same):
    part = [pl.ds(pl.multiple_of(n * 512 + g * 128, 128), 128) for n in range(3)]
    query, key, value = [qkv[:, p] for p in part]
    query = query * (head_inverse(query, ones) * scale_ref[:, part[0]])
    k_high, k_low = split(key * head_inverse(key, ones))
    keys = jnp.concatenate([k_high, k_high, k_low], axis=1)
    value = value.astype(BF16)
    values = jnp.concatenate([value, jnp.ones_like(value)], axis=1)
    head = lax.shift_right_logical(lax.broadcasted_iota(jnp.int32, query.shape, 1), 5)
    top, bottom = jnp.zeros_like(query), jnp.ones_like(query)
    for i in range(4):
        q_high, q_low = split(jnp.where(head == i, query, 0.0))
        scores = dot_nt(jnp.concatenate([q_high, q_low, q_high], axis=1), keys)
        weights = (jnp.exp(scores) * same).astype(BF16)
        out = dot(weights, values)
        top = jnp.where(head == i, out[:, :128], top)
        bottom = jnp.where(head == i, out[:, 128:], bottom)
    joined[:, part[0]] = (top / bottom).astype(BF16)


def block_kernel(
    tok_ref, cot_ref, ids_ref, scale_ref, router_ref, wqkv_any, wproj_any, wup_any, wdown_any,
    mixed_ref, oup_ref, odown_ref,
    wqkv, wproj, wup, wdown,
    resid, nsend, region, qkv, joined, attb, homeb, place, place_t, normed2, gate_s,
    send, csend, recv, cotr, rgrad, rows_t, hidden, gact, back,
    us, u1, u2, uh, ds, d1, d2, dh,
    wsem, hs, hr, ks, kr, xs, xr, cs, cr, bs, br, *sems,
):
    me, sy = lax.axis_index("sx"), lax.axis_index("sy")
    n_sy = lax.axis_size("sy")
    x, y, to_x, to_y = ring_places()
    rows_out = Exchange(me, True, lambda s, p: send.at[p], lambda s, m: recv.at[:, s], xs, xr)
    cots_out = Exchange(me, True, lambda s, p: csend.at[p], lambda s, m: cotr.at[:, s], cs, cr)
    home = Exchange(me, False, lambda s, p: csend.at[s], lambda s, m: back.at[m], bs, br)
    below, above = lax.rem(sy + 1, n_sy), lax.rem(sy + n_sy - 1, n_sy)
    after, before = lax.rem(me + 1, N_SX), lax.rem(me + N_SX - 1, N_SX)
    onward = [{"sy": below}] * 3 + [{"sx": after}, {"sy": below, "sx": after}]
    backward = [{"sy": above}] * 3 + [{"sx": before}, {"sy": above, "sx": before}]
    greeted = [{"sx": rows_out.peer(s)} for s in range(1, N_SX)] + to_x + to_y
    greeted += [onward[0], onward[4], backward[0], backward[4]]
    barrier = pltpu.get_barrier_semaphore()
    for target in greeted:
        pl.semaphore_signal(barrier, inc=1, device_id=target, device_id_type=MESH)

    loads = [
        pltpu.make_async_copy(wqkv_any, wqkv, wsem.at[0]),
        pltpu.make_async_copy(wproj_any, wproj, wsem.at[1]),
        pltpu.make_async_copy(wup_any, wup, wsem.at[2]),
        pltpu.make_async_copy(wdown_any, wdown, wsem.at[3]),
    ]
    for load in loads:
        load.start()

    places = ((1, 0), (2, 0), (3, 0), (0, 1), (0, 0))

    def tile_at(cg, rh):
        return (slice(8 * rh, 8 * rh + 8), slice(8 * cg, 8 * cg + 8))

    resid[...] = tok_ref[...].astype(F32)
    for piece, (cg, rh) in enumerate(places):
        from_cg, from_rh = (cg + 3) % 4, 1 - rh
        block = layer_norm(resid[tile_at(from_cg, from_rh)].reshape(64, 512))
        nsend[piece] = block.astype(BF16)
    for cg in range(1, 4):
        block = layer_norm(resid[tile_at(cg - 1, 0)].reshape(64, 512))
        region[cg, 1] = block.astype(BF16)

    def halo(piece, forward):
        cg, rh = places[piece]
        return pltpu.make_async_remote_copy(
            src_ref=nsend.at[piece] if forward else attb.at[cg, rh],
            dst_ref=region.at[cg, rh] if forward else homeb.at[piece],
            send_sem=(hs if forward else ks).at[piece],
            recv_sem=(hr if forward else kr).at[piece],
            device_id=(onward if forward else backward)[piece],
            device_id_type=MESH,
        )

    pl.semaphore_wait(barrier, len(greeted))
    for piece in (1, 2, 0, 4, 3):
        halo(piece, True).start()

    ids = ids_ref[...]
    named = lax.broadcasted_iota(jnp.int32, (512, 32), 1) == ids
    earlier = lax.broadcasted_iota(jnp.int32, (512, 512), 0) > lax.broadcasted_iota(
        jnp.int32, (512, 512), 1
    )
    counts = dot(jnp.where(earlier, 1.0, 0.0).astype(BF16), jnp.where(named, 1.0, 0.0).astype(BF16))
    rank = jnp.sum(jnp.where(named, counts, 0.0), axis=1, keepdims=True)
    slot = ids.astype(F32) * float(CAP) + rank
    for c in range(4):
        here = (lax.broadcasted_iota(jnp.int32, (512, 256), 1) + 256 * c).astype(F32)
        picked = jnp.where(here == slot, 1.0, 0.0).astype(BF16)
        place_t[:, 256 * c : 256 * c + 256] = picked
        place[256 * c : 256 * c + 256] = picked.T

    def gather(c, rows_ref, out_ref):
        rows = dot(place[256 * c : 256 * c + 256], rows_ref[...]).astype(BF16)
        out_ref[4 * c : 4 * c + 4] = rows.reshape(4, 2, CAP, 512)

    for c in range(4):
        gather(c, cot_ref, csend)
    for s in range(1, N_SX):
        cots_out.copy(s).start()
    cotr[:, 0] = csend[me]

    lane = lax.shift_right_logical(lax.broadcasted_iota(jnp.int32, (256, 128), 1), 5)
    row = lax.shift_right_logical(
        jnp.bitwise_and(lax.broadcasted_iota(jnp.int32, (256, 128), 0), 127), 5
    )
    ones = jnp.where(lane == row, 1.0, 0.0).astype(BF16)

    loads[0].wait()
    loads[1].wait()
    row_cut = jnp.where(sy == 0, 1, 0)
    for w in (1, 0):
        for piece in (1, 2) if w else (0, 4, 3):
            halo(piece, True).wait_recv()
        qkv[...] = dot(region[2 * w : 2 * w + 2].reshape(256, 512), wqkv[...])
        col_cut = jnp.where(me == 0, 1 - w, 0)

        def label(axis):
            b = lax.shift_right_logical(lax.broadcasted_iota(jnp.int32, (256, 256), axis), 6)
            return jnp.bitwise_and(b, 1) * (2 * row_cut) + lax.shift_right_logical(b, 1) * col_cut

        same = jnp.where(label(0) == label(1), 1.0, 0.0)

        def group(g, carry):
            attend_group(qkv, joined, g, scale_ref, ones, same)
            return carry

        lax.fori_loop(0, 4, group, 0)
        attended = dot(joined[...], wproj[...]).astype(BF16)
        attb[2 * w : 2 * w + 2] = attended.reshape(2, 2, 64, 512)
        for piece in (1, 2) if w else (0, 4, 3):
            halo(piece, False).start()
        for cg in (2, 3) if w else (1,):
            resid[tile_at(cg - 1, 0)] += attb[cg, 1].astype(F32).reshape(8, 8, 512)
    for piece in (1, 2, 0, 4, 3):
        cg, rh = places[piece]
        halo(piece, False).wait_recv()
        at = tile_at((cg + 3) % 4, 1 - rh)
        resid[at] += homeb[piece].astype(F32).reshape(8, 8, 512)
    for c in range(4):
        rows = layer_norm(resid[4 * c : 4 * c + 4].reshape(128, 512))
        normed2[128 * c : 128 * c + 128] = rows.astype(BF16)
    for c in range(4):
        gather(c, normed2, send)
    for s in range(1, N_SX):
        rows_out.copy(s).start()
    recv[:, 0] = send[me]
    logits = dot(normed2[...], router_ref[...])
    gate_s[...] = jax.nn.sigmoid(jnp.sum(jnp.where(named, logits, 0.0), axis=1, keepdims=True))
    loads[2].wait()
    loads[3].wait()
    for s in range(1, N_SX):
        cots_out.copy(s).wait_send()
    def hidden_part(g):
        for s in range(max(1, 8 * g), 8 * g + 8):
            rows_out.copy(s).wait_recv()
            cots_out.copy(s).wait_recv()
        for e in range(2):
            rows = recv[e, 8 * g : 8 * g + 8].reshape(256, 512)
            cot = cotr[e, 8 * g : 8 * g + 8].reshape(256, 512)
            logits = dot(rows, router_ref[...])
            column = lax.broadcasted_iota(jnp.int32, logits.shape, 1) == 2 * me + e
            gate = jax.nn.sigmoid(jnp.sum(jnp.where(column, logits, 0.0), axis=1, keepdims=True))
            grad = (gate * cot.astype(F32)).astype(BF16)
            rgrad[e, 256 * g : 256 * g + 256] = grad
            rows_t[e, :, 256 * g : 256 * g + 256] = rows.T

            def step(f, carry):
                part = pl.ds(pl.multiple_of(f * 512, 512), 512)
                act = dot(rows, wup[e, :, part])
                hid, slope = gelu_parts(act)
                hidden[e, 256 * g : 256 * g + 256, part] = hid.astype(BF16)
                through = dot_nt(grad, wdown[e, part, :])
                gact[e, 256 * g : 256 * g + 256, part] = (through * slope).astype(BF16)
                return carry

            lax.fori_loop(0, 4, step, 0)

    def return_part(g):
        for e in range(2):
            out = dot(hidden[e, 256 * g : 256 * g + 256], wdown[e]).astype(BF16)
            csend[8 * g : 8 * g + 8, e] = out.reshape(8, CAP, 512)
        for s in range(8 * g, 8 * g + 8):
            if s:
                home.copy(s).start()
        if g == 0:
            back[me] = csend[0]

    def up_block(e, ix, iy):
        col = pl.multiple_of(shard_of(ix, iy) * 128, 128)
        return dot(rows_t[e], gact[e, :, pl.ds(col, 128)])

    def down_block(e, iy, ix):
        col = pl.multiple_of(shard_of(ix, iy) * 128, 128)
        return dot_tn(hidden[e, :, pl.ds(col, 128)], rgrad[e])

    halves = (
        RingHalf(up_block, x, y, to_x, to_y, us, u1, u2, uh, oup_ref, sems[:4]),
        RingHalf(down_block, y, x, to_y, to_x, ds, d1, d2, dh, odown_ref, sems[4:]),
    )

    def each(method):
        def step(k, carry):
            for half in halves:
                getattr(half, method)(k)
            return carry

        lax.fori_loop(0, 4, step, 0)

    hidden_part(0)
    return_part(0)
    hidden_part(1)
    each("send_far")
    return_part(1)
    each("send_raw")
    each("pass_on")
    for k in range(4):
        for half in halves:
            half.close1(k)
    for half in halves:
        half.pass_on2()
    for s in range(1, N_SX):
        home.copy(s).wait_recv()
    moe = dot(place_t[...], back[...].reshape(1024, 512))
    mixed_ref[...] = (resid[...].reshape(512, 512) + gate_s[...] * moe).astype(BF16)
    for half in halves:
        half.close2()
    for half in halves:
        half.finish()
    for s in range(1, N_SX):
        rows_out.copy(s).wait_send()
        home.copy(s).wait_send()
    for piece in range(5):
        halo(piece, True).wait_send()
        halo(piece, False).wait_send()


def on_device(tokens, cotangent, w_qkv, w_proj, logit_scale, w_router, w_up, w_down, expert_ids):
    dma = pltpu.SemaphoreType.DMA
    vmem = pl.BlockSpec(memory_space=pltpu.VMEM)
    anywhere = pl.BlockSpec(memory_space=pl.ANY)
    ring = [dma((3, 2, 4)), dma((3, 2, 4)), dma((3, 2)), dma((3, 2))]
    buffers = [
        ((512, 1536), BF16),
        ((512, 512), BF16),
        ((2, 512, 2048), BF16),
        ((2, 2048, 512), BF16),
        ((16, 32, 512), F32),
        ((5, 64, 512), BF16),
        ((4, 2, 64, 512), BF16),
        ((256, 1536), F32),
        ((256, 512), BF16),
        ((4, 2, 64, 512), BF16),
        ((5, 64, 512), BF16),
        ((1024, 512), BF16),
        ((512, 1024), BF16),
        ((512, 512), BF16),
        ((512, 1), F32),
        ((N_SX, 2, CAP, 512), BF16),
        ((N_SX, 2, CAP, 512), BF16),
        ((2, N_SX, CAP, 512), BF16),
        ((2, N_SX, CAP, 512), BF16),
        ((2, 512, 512), BF16),
        ((2, 512, 512), BF16),
        ((2, 512, 2048), BF16),
        ((2, 512, 2048), BF16),
        ((N_SX, 2, CAP, 512), BF16),
        ((2, 2, 4, 512, 128), BF16),
        ((3, 2, 4, 512, 128), BF16),
        ((3, 2, 512, 128), BF16),
        ((3, 2, 512, 128), BF16),
        ((2, 2, 4, 128, 512), BF16),
        ((3, 2, 4, 128, 512), BF16),
        ((3, 2, 128, 512), BF16),
        ((3, 2, 128, 512), BF16),
    ]
    scale = jnp.repeat(logit_scale, 32)[None, :]
    mixed, grad_up, grad_down = pl.pallas_call(
        block_kernel,
        out_shape=(
            jax.ShapeDtypeStruct((512, 512), BF16),
            jax.ShapeDtypeStruct((2, 512, 128), F32),
            jax.ShapeDtypeStruct((2, 128, 512), F32),
        ),
        in_specs=[vmem] * 5 + [anywhere] * 4,
        out_specs=(vmem,) * 3,
        scratch_shapes=[pltpu.VMEM(shape, kind) for shape, kind in buffers]
        + [dma((4,))]
        + [dma((5,))] * 4
        + [dma((N_SX,))] * 6
        + ring * 2,
        compiler_params=pltpu.CompilerParams(
            collective_id=0, has_side_effects=True, vmem_limit_bytes=VMEM_MIB * 1024 * 1024
        ),
        name="block",
    )(
        tokens[0],
        cotangent.reshape(512, 512),
        expert_ids.reshape(512, 1),
        scale,
        w_router,
        w_qkv,
        w_proj,
        w_up,
        w_down,
    )
    return (mixed.reshape(1, 16, 32, 512), grad_up, grad_down)


def solution(mesh):
    return jax.shard_map(
        on_device,
        mesh=mesh,
        in_specs=(
            P("dp", "sy", "sx", None),
            P("dp", "sy", "sx", None),
            P(),
            P(),
            P(),
            P(),
            P("sx", None, None),
            P("sx", None, None),
            P("dp", "sy", "sx", None, None),
        ),
        out_specs=(
            P("dp", "sy", "sx", None),
            P("sx", None, ("sy", "dp")),
            P("sx", ("sy", "dp"), None),
        ),
        check_vma=False,
    )
```

time: 167 us -> 121 us (0.72); the launches traced: 164 us -> 121 us
  matrix products: 16 us -> 0 us
  starting transfers between devices: 12.4 us -> 0 us
  other arithmetic: 7.31 us -> 0 us
  local copies, waits for them, and re-layouts: 11.3 us -> 4.89 us
  waiting for transfers between devices: 6.04 us -> 0 us
  Pallas kernels: 110 us -> 115 us
    dot_general x7 -> x0, matrix products: 16 us -> none  [the longest x1 8.57 us: attend(): jnp.einsum('wqhc,wkhc->whqk', query, keys, precision=lax.Precision.HIGHEST)]
    ppermute x4 -> x0, starting transfers between devices: 12.4 us -> none  [from_behind(): return lax.ppermute(block, axis, route)]
    ppermute x4 -> x0, waiting for transfers between devices: 6.04 us -> none  [from_behind(): return lax.ppermute(block, axis, route)]
    pallas_call x1, Pallas kernels: 110 us -> 115 us  [on_device(): pl.pallas_call(block_kernel, out_shape=(jax.ShapeDtypeStruct((512, 512),...]
    unnamed x18 -> x4, local copies, waits for them, and re-layouts: 8.22 us -> 3.26 us
    convert_element_type x3 -> x0, other arithmetic: 2.3 us -> none  [the longest x1 1.4 us: on_device(): (slot[None, :] == jnp.arange(slots, dtype=jnp.int32)[:, None]).astype(jnp...]
    reduce_sum x6 -> x0, other arithmetic: 2.15 us -> none  [the longest x1 0.79 us: on_device(): rank = jnp.sum(jnp.where(onehot, running, 0), axis=-1)]
  transfers between devices with their start and end apart: 4 -> 0, of which waited for: 3 -> 0; matrix products, arithmetic and copies ran while one was open for 5% -> 0% of each run, Pallas kernels for 0% -> 0%
where the time goes in v3:
time: 121 us
  Pallas kernels  115 us (95%)
  local copies, waits for them, and re-layouts  4.89 us (4%)
    pallas_call x1, Pallas kernels, on_device(): pl.pallas_call(block_kernel, out_shape=(jax.ShapeDtypeStruct((512, 512),...  115 us
    unnamed x4, local copies, waits for them, and re-layouts  3.26 us

profile of v3, /device:TPU:1, one launch (start us, length us, event | category | flops | bytes accessed | tf_op | source)
XLA Modules:
  0.0 120.8 jit_solution(12901120170556967302)
XLA Ops:
  0.6 0.7 broadcast_in_dim.3
  1.4 0.1 broadcast_in_dim_reshape.3.scale_ref
  1.4 0.9 copy.14.router_ref
  2.3 0.8 copy.13.ids_ref
  3.2 115.3 %block.1 = (bf16[512,512]{1,0:T(8,128)(2,1)S(1)}, f32[2,512,128]{2,1,0:T(8,128)S(1)}, f32[2,128,512]{2,1,0:T(8,128)S(1)}) custom-call(bf16[16,32,512]{2,1,0:T(8,128)(2,1)} %bitcast.5, bf16[512,512]{1,0:T(8,128)(2,1)} %bitcast.6, s32[512,1]{1,0:T(8,128)S(1)} %copy.13.ids_ref, f32[1,512]{1,0:T(1,128)S(1)} %broadcast_in_dim_reshape.3.scale_ref, ...), custom_call_target="tpu_custom_call" | custom-call | tf_op jit(solution)/shard_map/block/pallas_call | solution.py:476
  118.4 0.8 copy.18
  119.2 0.8 copy.19
  120.0 0.8 copy.20

commit v4 on v3

--- a/solution.py
+++ b/solution.py
@@ -42,14 +42,13 @@
 
 
 class RingHalf:
-    def __init__(self, block, here_a, here_b, to_a, to_b, stage, bufs1, bufs2, hold, out, sems):
-        self.block = block
+    def __init__(self, full, part, cut, here_a, here_b, to_a, to_b, refs, out_at):
+        self.full, self.part, self.cut = full, part, cut
         self.pa, self.pb = here_a, here_b
         self.to_a, self.to_b = to_a, to_b
-        self.stage, self.bufs1, self.bufs2 = stage, bufs1, bufs2
-        self.hold = hold
-        self.out = out
-        self.s1, self.r1, self.s2, self.r2 = sems
+        self.stage, self.bufs1, self.bufs2, self.hold = refs[:4]
+        self.s1, self.r1, self.s2, self.r2 = refs[4:]
+        self.out_at = out_at
 
     def order(self, k):
         return lax.rem(self.pb + 2 + k + (k // 2) * (1 + 2 * (k % 2)), 4)
@@ -84,36 +83,34 @@
     def ahead(self, way):
         return lax.rem(self.pa + (1 if way == 0 else 3), 4)
 
-    def send_far(self, k):
+    def send_own(self, k):
+        far = self.full(lax.rem(self.pa + 2, 4), self.order(k)).astype(BF16)
         for way in range(2):
-            part = self.block(way, lax.rem(self.pa + 2, 4), self.order(k))
-            self.stage[0, way, k] = part.astype(BF16)
+            self.stage[0, way, k] = self.cut(far, way)
             self.copy1(0, way, k).start()
-
-    def send_raw(self, k):
         for way in range(2):
-            part = self.block(1 - way, self.ahead(way), self.order(k))
+            part = self.part(1 - way, self.ahead(way), self.order(k))
             self.stage[1, way, k] = part.astype(BF16)
             self.copy1(1, way, k).start()
 
     def pass_on(self, k):
         for way in range(2):
-            mine = self.block(way, self.ahead(way), self.order(k))
+            mine = self.part(way, self.ahead(way), self.order(k))
             self.copy1(0, way, k).wait_recv()
             self.bufs1[0, way, k] = (self.bufs1[0, way, k].astype(F32) + mine).astype(BF16)
             self.copy1(2, way, k).start()
 
     def close1(self, k):
-        for e in range(2):
-            total = self.block(e, self.pa, self.order(k))
-            self.copy1(1, 1 - e, k).wait_recv()
-            self.copy1(2, e, k).wait_recv()
-            total = total + self.bufs1[1, 1 - e, k].astype(F32)
-            total = total + self.bufs1[2, e, k].astype(F32)
+        own = self.full(self.pa, self.order(k))
+        for h in range(2):
+            self.copy1(1, 1 - h, k).wait_recv()
+            self.copy1(2, h, k).wait_recv()
+            total = self.cut(own, h) + self.bufs1[1, 1 - h, k].astype(F32)
+            total = total + self.bufs1[2, h, k].astype(F32)
             if k < 3:
-                self.hold[k, e] = total.astype(BF16)
+                self.hold[k, h] = total.astype(BF16)
             else:
-                self.out[e] = total
+                self.out_at(h)[...] = total
         if k == 0:
             self.copy2(0, 0).start()
             self.copy2(0, 1).start()
@@ -130,11 +127,11 @@
             self.copy2(2, way).start()
 
     def close2(self):
-        for e in range(2):
-            self.copy2(1, 1 - e).wait_recv()
-            self.copy2(2, e).wait_recv()
-            total = self.out[e] + self.bufs2[1, 1 - e].astype(F32)
-            self.out[e] = total + self.bufs2[2, e].astype(F32)
+        for h in range(2):
+            self.copy2(1, 1 - h).wait_recv()
+            self.copy2(2, h).wait_recv()
+            out = self.out_at(h)
+            out[...] = out[...] + self.bufs2[1, 1 - h].astype(F32) + self.bufs2[2, h].astype(F32)
 
     def finish(self):
         for kind in range(3):
@@ -154,13 +151,13 @@
         d = NEAR_FIRST[slot]
         return lax.rem(self.me + (d if self.away else N_SX - d), N_SX)
 
-    def copy(self, slot):
+    def copy(self, slot, e):
         peer = self.peer(slot)
         return pltpu.make_async_remote_copy(
-            src_ref=self.source(slot, peer),
-            dst_ref=self.landing(slot, self.me),
-            send_sem=self.send_sem.at[slot],
-            recv_sem=self.recv_sem.at[slot],
+            src_ref=self.source(slot, peer, e),
+            dst_ref=self.landing(slot, self.me, e),
+            send_sem=self.send_sem.at[e, slot],
+            recv_sem=self.recv_sem.at[e, slot],
             device_id={"sx": peer},
             device_id_type=MESH,
         )
@@ -194,7 +191,7 @@
 def attend_group(qkv, joined, g, scale_ref, ones, same):
     part = [pl.ds(pl.multiple_of(n * 512 + g * 128, 128), 128) for n in range(3)]
     query, key, value = [qkv[:, p] for p in part]
-    query = query * (head_inverse(query, ones) * scale_ref[:, part[0]])
+    query = query * head_inverse(query, ones)
     k_high, k_low = split(key * head_inverse(key, ones))
     keys = jnp.concatenate([k_high, k_high, k_low], axis=1)
     value = value.astype(BF16)
@@ -202,7 +199,7 @@
     head = lax.shift_right_logical(lax.broadcasted_iota(jnp.int32, query.shape, 1), 5)
     top, bottom = jnp.zeros_like(query), jnp.ones_like(query)
     for i in range(4):
-        q_high, q_low = split(jnp.where(head == i, query, 0.0))
+        q_high, q_low = split(jnp.where(head == i, query * scale_ref[4 * g + i], 0.0))
         scores = dot_nt(jnp.concatenate([q_high, q_low, q_high], axis=1), keys)
         weights = (jnp.exp(scores) * same).astype(BF16)
         out = dot(weights, values)
@@ -215,23 +212,23 @@
     tok_ref, cot_ref, ids_ref, scale_ref, router_ref, wqkv_any, wproj_any, wup_any, wdown_any,
     mixed_ref, oup_ref, odown_ref,
     wqkv, wproj, wup, wdown,
-    resid, nsend, region, qkv, joined, attb, homeb, place, place_t, normed2, gate_s,
+    resid, nsend, region, qkv, joined, attb, homeb, place, normed2,
     send, csend, recv, cotr, rgrad, rows_t, hidden, gact, back,
     us, u1, u2, uh, ds, d1, d2, dh,
-    wsem, hs, hr, ks, kr, xs, xr, cs, cr, bs, br, *sems,
+    wsem, near, hs, hr, ks, kr, xs, xr, cs, cr, bs, br, *sems,
 ):
     me, sy = lax.axis_index("sx"), lax.axis_index("sy")
     n_sy = lax.axis_size("sy")
     x, y, to_x, to_y = ring_places()
-    rows_out = Exchange(me, True, lambda s, p: send.at[p], lambda s, m: recv.at[:, s], xs, xr)
-    cots_out = Exchange(me, True, lambda s, p: csend.at[p], lambda s, m: cotr.at[:, s], cs, cr)
-    home = Exchange(me, False, lambda s, p: csend.at[s], lambda s, m: back.at[m], bs, br)
+    rows_out = Exchange(me, True, lambda s, p, e: send.at[e, p], lambda s, m, e: recv.at[e, s], xs, xr)
+    cots_out = Exchange(me, True, lambda s, p, e: csend.at[e, p], lambda s, m, e: cotr.at[e, s], cs, cr)
+    home = Exchange(me, False, lambda s, p, e: csend.at[e, s], lambda s, m, e: back.at[e, m], bs, br)
     below, above = lax.rem(sy + 1, n_sy), lax.rem(sy + n_sy - 1, n_sy)
     after, before = lax.rem(me + 1, N_SX), lax.rem(me + N_SX - 1, N_SX)
     onward = [{"sy": below}] * 3 + [{"sx": after}, {"sy": below, "sx": after}]
     backward = [{"sy": above}] * 3 + [{"sx": before}, {"sy": above, "sx": before}]
-    greeted = [{"sx": rows_out.peer(s)} for s in range(1, N_SX)] + to_x + to_y
-    greeted += [onward[0], onward[4], backward[0], backward[4]]
+    greeted = to_x + to_y + [onward[0], onward[3], onward[4]]
+    greeted += [backward[0], backward[3], backward[4]]
     barrier = pltpu.get_barrier_semaphore()
     for target in greeted:
         pl.semaphore_signal(barrier, inc=1, device_id=target, device_id_type=MESH)
@@ -274,29 +271,41 @@
     for piece in (1, 2, 0, 4, 3):
         halo(piece, True).start()
 
+    def tell(r):
+        for step in (2**r, N_SX - 2**r):
+            peer = {"sx": lax.rem(me + step, N_SX)}
+            pl.semaphore_signal(near.at[r], inc=1, device_id=peer, device_id_type=MESH)
+
+    tell(0)
+
     ids = ids_ref[...]
-    named = lax.broadcasted_iota(jnp.int32, (512, 32), 1) == ids
-    earlier = lax.broadcasted_iota(jnp.int32, (512, 512), 0) > lax.broadcasted_iota(
+    named = lax.broadcasted_iota(jnp.int32, (32, 512), 0) == ids
+    earlier = lax.broadcasted_iota(jnp.int32, (512, 512), 0) < lax.broadcasted_iota(
         jnp.int32, (512, 512), 1
     )
-    counts = dot(jnp.where(earlier, 1.0, 0.0).astype(BF16), jnp.where(named, 1.0, 0.0).astype(BF16))
-    rank = jnp.sum(jnp.where(named, counts, 0.0), axis=1, keepdims=True)
-    slot = ids.astype(F32) * float(CAP) + rank
+    counts = dot(jnp.where(named, 1.0, 0.0).astype(BF16), jnp.where(earlier, 1.0, 0.0).astype(BF16))
+    rank = jnp.sum(jnp.where(named, counts, 0.0), axis=0, keepdims=True)
+    slot = jnp.bitwise_and(ids, 1) * 512 + lax.shift_right_logical(ids, 1) * CAP
+    slot = slot.astype(F32) + rank
     for c in range(4):
-        here = (lax.broadcasted_iota(jnp.int32, (512, 256), 1) + 256 * c).astype(F32)
-        picked = jnp.where(here == slot, 1.0, 0.0).astype(BF16)
-        place_t[:, 256 * c : 256 * c + 256] = picked
-        place[256 * c : 256 * c + 256] = picked.T
-
-    def gather(c, rows_ref, out_ref):
-        rows = dot(place[256 * c : 256 * c + 256], rows_ref[...]).astype(BF16)
-        out_ref[4 * c : 4 * c + 4] = rows.reshape(4, 2, CAP, 512)
-
-    for c in range(4):
-        gather(c, cot_ref, csend)
-    for s in range(1, N_SX):
-        cots_out.copy(s).start()
-    cotr[:, 0] = csend[me]
+        here = (lax.broadcasted_iota(jnp.int32, (256, 512), 0) + 256 * c).astype(F32)
+        place[256 * c : 256 * c + 256] = jnp.where(here == slot, 1.0, 0.0).astype(BF16)
+    pl.semaphore_wait(near.at[0], 2)
+    tell(1)
+
+    def gather(e, rows_ref, out_ref):
+        rows = dot(place[512 * e : 512 * e + 512], rows_ref[...]).astype(BF16)
+        out_ref[e] = rows.reshape(N_SX, CAP, 512)
+
+    gather(0, cot_ref, csend)
+    pl.semaphore_wait(near.at[1], 2)
+    tell(2)
+    gather(1, cot_ref, csend)
+    pl.semaphore_wait(near.at[2], 2)
+    for e in range(2):
+        for s in range(1, N_SX):
+            cots_out.copy(s, e).start()
+        cotr[e, 0] = csend[e, me]
 
     lane = lax.shift_right_logical(lax.broadcasted_iota(jnp.int32, (256, 128), 1), 5)
     row = lax.shift_right_logical(
@@ -338,66 +347,78 @@
     for c in range(4):
         rows = layer_norm(resid[4 * c : 4 * c + 4].reshape(128, 512))
         normed2[128 * c : 128 * c + 128] = rows.astype(BF16)
-    for c in range(4):
-        gather(c, normed2, send)
-    for s in range(1, N_SX):
-        rows_out.copy(s).start()
-    recv[:, 0] = send[me]
-    logits = dot(normed2[...], router_ref[...])
-    gate_s[...] = jax.nn.sigmoid(jnp.sum(jnp.where(named, logits, 0.0), axis=1, keepdims=True))
+    for e in range(2):
+        gather(e, normed2, send)
+        for s in range(1, N_SX):
+            rows_out.copy(s, e).start()
+        recv[e, 0] = send[e, me]
     loads[2].wait()
     loads[3].wait()
-    for s in range(1, N_SX):
-        cots_out.copy(s).wait_send()
-    def hidden_part(g):
-        for s in range(max(1, 8 * g), 8 * g + 8):
-            rows_out.copy(s).wait_recv()
-            cots_out.copy(s).wait_recv()
-        for e in range(2):
-            rows = recv[e, 8 * g : 8 * g + 8].reshape(256, 512)
-            cot = cotr[e, 8 * g : 8 * g + 8].reshape(256, 512)
-            logits = dot(rows, router_ref[...])
-            column = lax.broadcasted_iota(jnp.int32, logits.shape, 1) == 2 * me + e
-            gate = jax.nn.sigmoid(jnp.sum(jnp.where(column, logits, 0.0), axis=1, keepdims=True))
-            grad = (gate * cot.astype(F32)).astype(BF16)
-            rgrad[e, 256 * g : 256 * g + 256] = grad
-            rows_t[e, :, 256 * g : 256 * g + 256] = rows.T
-
-            def step(f, carry):
-                part = pl.ds(pl.multiple_of(f * 512, 512), 512)
-                act = dot(rows, wup[e, :, part])
-                hid, slope = gelu_parts(act)
-                hidden[e, 256 * g : 256 * g + 256, part] = hid.astype(BF16)
-                through = dot_nt(grad, wdown[e, part, :])
-                gact[e, 256 * g : 256 * g + 256, part] = (through * slope).astype(BF16)
-                return carry
-
-            lax.fori_loop(0, 4, step, 0)
-
-    def return_part(g):
-        for e in range(2):
-            out = dot(hidden[e, 256 * g : 256 * g + 256], wdown[e]).astype(BF16)
-            csend[8 * g : 8 * g + 8, e] = out.reshape(8, CAP, 512)
-        for s in range(8 * g, 8 * g + 8):
-            if s:
-                home.copy(s).start()
-        if g == 0:
-            back[me] = csend[0]
-
-    def up_block(e, ix, iy):
-        col = pl.multiple_of(shard_of(ix, iy) * 128, 128)
-        return dot(rows_t[e], gact[e, :, pl.ds(col, 128)])
-
-    def down_block(e, iy, ix):
-        col = pl.multiple_of(shard_of(ix, iy) * 128, 128)
-        return dot_tn(hidden[e, :, pl.ds(col, 128)], rgrad[e])
-
-    halves = (
-        RingHalf(up_block, x, y, to_x, to_y, us, u1, u2, uh, oup_ref, sems[:4]),
-        RingHalf(down_block, y, x, to_y, to_x, ds, d1, d2, dh, odown_ref, sems[4:]),
-    )
-
-    def each(method):
+    for e in range(2):
+        for s in range(1, N_SX):
+            cots_out.copy(s, e).wait_send()
+
+    def hidden_part(e):
+        for s in range(1, N_SX):
+            cots_out.copy(s, e).wait_recv()
+            rows_out.copy(s, e).wait_recv()
+        rows = recv[e].reshape(512, 512)
+        logits = dot_nt(rows, router_ref[...])
+        column = lax.broadcasted_iota(jnp.int32, logits.shape, 1) == 2 * me + e
+        gate = jax.nn.sigmoid(jnp.sum(jnp.where(column, logits, 0.0), axis=1, keepdims=True))
+        rgrad[e] = (gate * cotr[e].reshape(512, 512).astype(F32)).astype(BF16)
+        rows_t[e] = rows.T
+
+        def step(f, carry):
+            part = pl.ds(pl.multiple_of(f * 256, 256), 256)
+            act = dot(recv[e].reshape(512, 512), wup[e, :, part])
+            hid, slope = gelu_parts(act)
+            hidden[e, :, part] = hid.astype(BF16)
+            through = dot_nt(rgrad[e], wdown[e, part, :])
+            gact[e, :, part] = (through * slope).astype(BF16)
+            return carry
+
+        lax.fori_loop(0, 8, step, 0)
+
+    def return_part(e):
+        out = dot(hidden[e], wdown[e]).astype(BF16)
+        csend[e] = out.reshape(N_SX, CAP, 512)
+        for s in range(1, N_SX):
+            home.copy(s, e).start()
+        back[e, me] = csend[e, 0]
+
+    def halves_of(e):
+        def columns(ix, iy):
+            return pl.ds(pl.multiple_of(shard_of(ix, iy) * 128, 128), 128)
+
+        def up_full(ix, iy):
+            return dot(rows_t[e], gact[e, :, columns(ix, iy)])
+
+        def up_part(h, ix, iy):
+            return dot(rows_t[e, 256 * h : 256 * h + 256], gact[e, :, columns(ix, iy)])
+
+        def down_full(iy, ix):
+            return dot_tn(hidden[e, :, columns(ix, iy)], rgrad[e])
+
+        def down_part(h, iy, ix):
+            return dot_tn(hidden[e, :, columns(ix, iy)], rgrad[e, :, 256 * h : 256 * h + 256])
+
+        up_refs = [ref.at[e] for ref in (us, u1, u2, uh) + sems[:4]]
+        down_refs = [ref.at[e] for ref in (ds, d1, d2, dh) + sems[4:]]
+        return (
+            RingHalf(
+                up_full, up_part, lambda v, h: v[256 * h : 256 * h + 256],
+                x, y, to_x, to_y, up_refs, lambda h: oup_ref.at[e, pl.ds(256 * h, 256)],
+            ),
+            RingHalf(
+                down_full, down_part, lambda v, h: v[:, 256 * h : 256 * h + 256],
+                y, x, to_y, to_x, down_refs, lambda h: odown_ref.at[e, :, pl.ds(256 * h, 256)],
+            ),
+        )
+
+    first, second = halves_of(0), halves_of(1)
+
+    def each(halves, method):
         def step(k, carry):
             for half in halves:
                 getattr(half, method)(k)
@@ -405,29 +426,44 @@
 
         lax.fori_loop(0, 4, step, 0)
 
+    def close(halves):
+        for k in range(4):
+            for half in halves:
+                half.close1(k)
+
     hidden_part(0)
+    each(first, "send_own")
+    each(first, "pass_on")
+    hidden_part(1)
+    each(second, "send_own")
+    close(first)
     return_part(0)
-    hidden_part(1)
-    each("send_far")
     return_part(1)
-    each("send_raw")
-    each("pass_on")
-    for k in range(4):
-        for half in halves:
-            half.close1(k)
-    for half in halves:
+    each(second, "pass_on")
+    for half in first:
         half.pass_on2()
-    for s in range(1, N_SX):
-        home.copy(s).wait_recv()
-    moe = dot(place_t[...], back[...].reshape(1024, 512))
-    mixed_ref[...] = (resid[...].reshape(512, 512) + gate_s[...] * moe).astype(BF16)
-    for half in halves:
+    close(second)
+    for half in second:
+        half.pass_on2()
+    logits = dot_nt(router_ref[...], normed2[...])
+    gate = jax.nn.sigmoid(jnp.sum(jnp.where(named, logits, 0.0), axis=0, keepdims=True))
+    same_token = lax.broadcasted_iota(jnp.int32, (512, 512), 0) == lax.broadcasted_iota(
+        jnp.int32, (512, 512), 1
+    )
+    gate = jnp.sum(jnp.where(same_token, gate, 0.0), axis=1, keepdims=True)
+    for e in range(2):
+        for s in range(1, N_SX):
+            home.copy(s, e).wait_recv()
+    moe = dot_tn(place[...], back[...].reshape(1024, 512))
+    mixed_ref[...] = (resid[...].reshape(512, 512) + gate * moe).astype(BF16)
+    for half in first + second:
         half.close2()
-    for half in halves:
+    for half in first + second:
         half.finish()
-    for s in range(1, N_SX):
-        rows_out.copy(s).wait_send()
-        home.copy(s).wait_send()
+    for e in range(2):
+        for s in range(1, N_SX):
+            rows_out.copy(s, e).wait_send()
+            home.copy(s, e).wait_send()
     for piece in range(5):
         halo(piece, True).wait_send()
         halo(piece, False).wait_send()
@@ -437,7 +473,7 @@
     dma = pltpu.SemaphoreType.DMA
     vmem = pl.BlockSpec(memory_space=pltpu.VMEM)
     anywhere = pl.BlockSpec(memory_space=pl.ANY)
-    ring = [dma((3, 2, 4)), dma((3, 2, 4)), dma((3, 2)), dma((3, 2))]
+    ring = [dma((2, 3, 2, 4)), dma((2, 3, 2, 4)), dma((2, 3, 2)), dma((2, 3, 2))]
     buffers = [
         ((512, 1536), BF16),
         ((512, 512), BF16),
@@ -451,28 +487,25 @@
         ((4, 2, 64, 512), BF16),
         ((5, 64, 512), BF16),
         ((1024, 512), BF16),
-        ((512, 1024), BF16),
         ((512, 512), BF16),
-        ((512, 1), F32),
-        ((N_SX, 2, CAP, 512), BF16),
-        ((N_SX, 2, CAP, 512), BF16),
+        ((2, N_SX, CAP, 512), BF16),
+        ((2, N_SX, CAP, 512), BF16),
         ((2, N_SX, CAP, 512), BF16),
         ((2, N_SX, CAP, 512), BF16),
         ((2, 512, 512), BF16),
         ((2, 512, 512), BF16),
         ((2, 512, 2048), BF16),
         ((2, 512, 2048), BF16),
-        ((N_SX, 2, CAP, 512), BF16),
-        ((2, 2, 4, 512, 128), BF16),
-        ((3, 2, 4, 512, 128), BF16),
-        ((3, 2, 512, 128), BF16),
-        ((3, 2, 512, 128), BF16),
-        ((2, 2, 4, 128, 512), BF16),
-        ((3, 2, 4, 128, 512), BF16),
-        ((3, 2, 128, 512), BF16),
-        ((3, 2, 128, 512), BF16),
+        ((2, N_SX, CAP, 512), BF16),
+        ((2, 2, 2, 4, 256, 128), BF16),
+        ((2, 3, 2, 4, 256, 128), BF16),
+        ((2, 3, 2, 256, 128), BF16),
+        ((2, 3, 2, 256, 128), BF16),
+        ((2, 2, 2, 4, 128, 256), BF16),
+        ((2, 3, 2, 4, 128, 256), BF16),
+        ((2, 3, 2, 128, 256), BF16),
+        ((2, 3, 2, 128, 256), BF16),
     ]
-    scale = jnp.repeat(logit_scale, 32)[None, :]
     mixed, grad_up, grad_down = pl.pallas_call(
         block_kernel,
         out_shape=(
@@ -480,12 +513,12 @@
             jax.ShapeDtypeStruct((2, 512, 128), F32),
             jax.ShapeDtypeStruct((2, 128, 512), F32),
         ),
-        in_specs=[vmem] * 5 + [anywhere] * 4,
+        in_specs=[vmem] * 3 + [pl.BlockSpec(memory_space=pltpu.SMEM), vmem] + [anywhere] * 4,
         out_specs=(vmem,) * 3,
         scratch_shapes=[pltpu.VMEM(shape, kind) for shape, kind in buffers]
-        + [dma((4,))]
+        + [dma((4,)), pltpu.SemaphoreType.REGULAR((3,))]
         + [dma((5,))] * 4
-        + [dma((N_SX,))] * 6
+        + [dma((2, N_SX))] * 6
         + ring * 2,
         compiler_params=pltpu.CompilerParams(
             collective_id=0, has_side_effects=True, vmem_limit_bytes=VMEM_MIB * 1024 * 1024
@@ -494,9 +527,9 @@
     )(
         tokens[0],
         cotangent.reshape(512, 512),
-        expert_ids.reshape(512, 1),
-        scale,
-        w_router,
+        expert_ids.reshape(1, 512),
+        logit_scale,
+        w_router.T,
         w_qkv,
         w_proj,
         w_up,

time: 121 us -> 129 us (1.066)
  Pallas kernels: 115 us -> 123 us
    pallas_call x1, Pallas kernels: 115 us -> 123 us  [on_device(): pl.pallas_call(block_kernel, out_shape=(jax.ShapeDtypeStruct((512, 512),...]
    unnamed x4 -> x9, local copies, waits for them, and re-layouts: 3.26 us -> 4.47 us
where the time goes in v4:
time: 129 us; the launch traced here: 128 us
  Pallas kernels  123 us (95%)
  local copies, waits for them, and re-layouts  4.47 us (3%)
    pallas_call x1, Pallas kernels, on_device(): pl.pallas_call(block_kernel, out_shape=(jax.ShapeDtypeStruct((512, 512),...  123 us
    unnamed x9, local copies, waits for them, and re-layouts  4.47 us

profile of v4, /device:TPU:1, one launch (start us, length us, event | category | flops | bytes accessed | tf_op | source)
XLA Modules:
  0.0 128.4 jit_solution(15846073657963654623)
XLA Ops:
  0.6 0.0 copy-start
  0.6 0.7 copy-done
  1.4 0.0 copy-start.1
  1.4 0.7 copy-done.1
  2.1 0.0 copy-start.2
  2.1 0.7 copy-done.2
  2.7 123.3 %block.1 = (bf16[512,512]{1,0:T(8,128)(2,1)S(1)}, f32[2,512,128]{2,1,0:T(8,128)S(1)}, f32[2,128,512]{2,1,0:T(8,128)S(1)}) custom-call(bf16[16,32,512]{2,1,0:T(8,128)(2,1)} %bitcast.8, bf16[512,512]{1,0:T(8,128)(2,1)} %bitcast.9, s32[1,512]{1,0:T(1,128)S(1)} %bitcast.7, f32[16]{0:T(128)S(1)} %copy-done.2, bf16[32,512]{1,0:T(8,128)(2,1)S(1)} %bitcast.6, ...), custom_call_target="tpu_custom_call" | custom-call | tf_op jit(solution)/shard_map/block/pallas_call | solution.py:509
  126.0 0.8 copy.15
  126.8 0.8 copy.16
  127.6 0.8 copy.17
Async XLA Ops:
  0.6 0.8 copy-start
  1.4 0.7 copy-start.1
  2.1 0.7 copy-start.2

commit v5 on v4

--- a/solution.py
+++ b/solution.py
@@ -42,24 +42,34 @@
 
 
 class RingHalf:
-    def __init__(self, full, part, cut, here_a, here_b, to_a, to_b, refs, out_at):
-        self.full, self.part, self.cut = full, part, cut
+    def __init__(self, fill, here_a, here_b, to_a, to_b, refs, out_at):
+        self.fill = fill
         self.pa, self.pb = here_a, here_b
         self.to_a, self.to_b = to_a, to_b
-        self.stage, self.bufs1, self.bufs2, self.hold = refs[:4]
+        self.mine, self.bufs1, self.bufs2, self.hold = refs[:4]
         self.s1, self.r1, self.s2, self.r2 = refs[4:]
         self.out_at = out_at
 
-    def order(self, k):
-        return lax.rem(self.pb + 2 + k + (k // 2) * (1 + 2 * (k % 2)), 4)
-
-    def copy1(self, kind, way, k):
-        ref = self.bufs1.at[0, way, k] if kind == 2 else self.stage.at[kind, way, k]
+    def rank_of(self, ib):
+        d = lax.rem(ib - self.pb + 4, 4)
+        return (d // 2) * (d - 2) + (1 - d // 2) * (3 - d)
+
+    def chunk(self, d):
+        self.fill(self.mine.at[d], lax.rem(self.pa + d, 4), self.rank_of)
+
+    def copy1(self, kind, way, kk):
+        two = pl.ds(2 * kk, 2)
+        if kind == 0:
+            ref = self.mine.at[2, way, two]
+        elif kind == 1:
+            ref = self.mine.at[1 + 2 * way, 1 - way, two]
+        else:
+            ref = self.bufs1.at[0, way, two]
         return pltpu.make_async_remote_copy(
             src_ref=ref,
-            dst_ref=self.bufs1.at[kind, way, k],
-            send_sem=self.s1.at[kind, way, k],
-            recv_sem=self.r1.at[kind, way, k],
+            dst_ref=self.bufs1.at[kind, way, two],
+            send_sem=self.s1,
+            recv_sem=self.r1.at[kind, way, kk],
             device_id=self.to_a[way],
             device_id_type=MESH,
         )
@@ -74,56 +84,60 @@
         return pltpu.make_async_remote_copy(
             src_ref=ref,
             dst_ref=self.bufs2.at[kind, way],
-            send_sem=self.s2.at[kind, way],
+            send_sem=self.s2,
             recv_sem=self.r2.at[kind, way],
             device_id=self.to_b[way],
             device_id_type=MESH,
         )
 
-    def ahead(self, way):
-        return lax.rem(self.pa + (1 if way == 0 else 3), 4)
-
-    def send_own(self, k):
-        far = self.full(lax.rem(self.pa + 2, 4), self.order(k)).astype(BF16)
+    def send_far(self):
+        self.chunk(2)
+        for kk in range(2):
+            for way in range(2):
+                self.copy1(0, way, kk).start()
+
+    def send_raw(self):
         for way in range(2):
-            self.stage[0, way, k] = self.cut(far, way)
-            self.copy1(0, way, k).start()
+            self.chunk(1 + 2 * way)
+            for kk in range(2):
+                self.copy1(1, way, kk).start()
+
+    def keep_own(self):
+        self.chunk(0)
+
+    def pass_on(self, kk):
         for way in range(2):
-            part = self.part(1 - way, self.ahead(way), self.order(k))
-            self.stage[1, way, k] = part.astype(BF16)
-            self.copy1(1, way, k).start()
-
-    def pass_on(self, k):
-        for way in range(2):
-            mine = self.part(way, self.ahead(way), self.order(k))
-            self.copy1(0, way, k).wait_recv()
-            self.bufs1[0, way, k] = (self.bufs1[0, way, k].astype(F32) + mine).astype(BF16)
-            self.copy1(2, way, k).start()
-
-    def close1(self, k):
-        own = self.full(self.pa, self.order(k))
+            self.copy1(0, way, kk).wait_recv()
+            for k in (2 * kk, 2 * kk + 1):
+                own = self.mine[1 + 2 * way, way, k].astype(F32)
+                self.bufs1[0, way, k] = (self.bufs1[0, way, k].astype(F32) + own).astype(BF16)
+            self.copy1(2, way, kk).start()
+
+    def close1(self, kk):
         for h in range(2):
-            self.copy1(1, 1 - h, k).wait_recv()
-            self.copy1(2, h, k).wait_recv()
-            total = self.cut(own, h) + self.bufs1[1, 1 - h, k].astype(F32)
-            total = total + self.bufs1[2, h, k].astype(F32)
-            if k < 3:
-                self.hold[k, h] = total.astype(BF16)
-            else:
-                self.out_at(h)[...] = total
-        if k == 0:
-            self.copy2(0, 0).start()
-            self.copy2(0, 1).start()
-        elif k == 1:
-            self.copy2(1, 1).start()
-        elif k == 2:
-            self.copy2(1, 0).start()
+            self.copy1(1, 1 - h, kk).wait_recv()
+            self.copy1(2, h, kk).wait_recv()
+        for k in (2 * kk, 2 * kk + 1):
+            for h in range(2):
+                total = self.mine[0, h, k].astype(F32) + self.bufs1[1, 1 - h, k].astype(F32)
+                total = total + self.bufs1[2, h, k].astype(F32)
+                if k < 3:
+                    self.hold[k, h] = total.astype(BF16)
+                else:
+                    self.out_at(h)[...] = total
+            if k == 0:
+                self.copy2(0, 0).start()
+                self.copy2(0, 1).start()
+            elif k == 1:
+                self.copy2(1, 1).start()
+            elif k == 2:
+                self.copy2(1, 0).start()
 
     def pass_on2(self):
         for way in range(2):
             self.copy2(0, way).wait_recv()
-            mine = self.hold[2 - way, way].astype(F32)
-            self.bufs2[0, way] = (self.bufs2[0, way].astype(F32) + mine).astype(BF16)
+            own = self.hold[2 - way, way].astype(F32)
+            self.bufs2[0, way] = (self.bufs2[0, way].astype(F32) + own).astype(BF16)
             self.copy2(2, way).start()
 
     def close2(self):
@@ -134,11 +148,8 @@
             out[...] = out[...] + self.bufs2[1, 1 - h].astype(F32) + self.bufs2[2, h].astype(F32)
 
     def finish(self):
-        for kind in range(3):
-            for way in range(2):
-                for k in range(4):
-                    self.copy1(kind, way, k).wait_send()
-                self.copy2(kind, way).wait_send()
+        pltpu.make_async_copy(self.bufs1, self.bufs1, self.s1).wait()
+        pltpu.make_async_copy(self.bufs2, self.bufs2, self.s2).wait()
 
 
 class Exchange:
@@ -151,16 +162,20 @@
         d = NEAR_FIRST[slot]
         return lax.rem(self.me + (d if self.away else N_SX - d), N_SX)
 
-    def copy(self, slot, e):
-        peer = self.peer(slot)
-        return pltpu.make_async_remote_copy(
-            src_ref=self.source(slot, peer, e),
-            dst_ref=self.landing(slot, self.me, e),
-            send_sem=self.send_sem.at[e, slot],
-            recv_sem=self.recv_sem.at[e, slot],
-            device_id={"sx": peer},
-            device_id_type=MESH,
-        )
+    def start(self):
+        for slot in range(1, N_SX):
+            peer = self.peer(slot)
+            pltpu.make_async_remote_copy(
+                src_ref=self.source(slot, peer),
+                dst_ref=self.landing(slot, self.me),
+                send_sem=self.send_sem,
+                recv_sem=self.recv_sem,
+                device_id={"sx": peer},
+                device_id_type=MESH,
+            ).start()
+
+    def wait(self, whole, sem):
+        pltpu.make_async_copy(whole, whole, sem).wait()
 
 
 def gelu_parts(v):
@@ -215,20 +230,31 @@
     resid, nsend, region, qkv, joined, attb, homeb, place, normed2,
     send, csend, recv, cotr, rgrad, rows_t, hidden, gact, back,
     us, u1, u2, uh, ds, d1, d2, dh,
-    wsem, near, hs, hr, ks, kr, xs, xr, cs, cr, bs, br, *sems,
+    wsem, hs, hr, ks, kr, xs, xr, cs, cr, bs, br, *sems,
 ):
     me, sy = lax.axis_index("sx"), lax.axis_index("sy")
     n_sy = lax.axis_size("sy")
     x, y, to_x, to_y = ring_places()
-    rows_out = Exchange(me, True, lambda s, p, e: send.at[e, p], lambda s, m, e: recv.at[e, s], xs, xr)
-    cots_out = Exchange(me, True, lambda s, p, e: csend.at[e, p], lambda s, m, e: cotr.at[e, s], cs, cr)
-    home = Exchange(me, False, lambda s, p, e: csend.at[e, s], lambda s, m, e: back.at[e, m], bs, br)
+    rows_out = [
+        Exchange(
+            me, True,
+            lambda s, p, e=e: send.at[e, p], lambda s, m, e=e: recv.at[e, s], xs.at[e], xr.at[e],
+        )
+        for e in range(2)
+    ]
+    cots_out = Exchange(
+        me, True, lambda s, p: csend.at[:, p], lambda s, m: cotr.at[:, s], cs.at[0], cr.at[0]
+    )
+    home = Exchange(
+        me, False, lambda s, p: csend.at[:, s], lambda s, m: back.at[:, m], bs.at[0], br.at[0]
+    )
+    others = pl.ds(1, N_SX - 1)
     below, above = lax.rem(sy + 1, n_sy), lax.rem(sy + n_sy - 1, n_sy)
     after, before = lax.rem(me + 1, N_SX), lax.rem(me + N_SX - 1, N_SX)
     onward = [{"sy": below}] * 3 + [{"sx": after}, {"sy": below, "sx": after}]
     backward = [{"sy": above}] * 3 + [{"sx": before}, {"sy": above, "sx": before}]
-    greeted = to_x + to_y + [onward[0], onward[3], onward[4]]
-    greeted += [backward[0], backward[3], backward[4]]
+    greeted = [{"sx": rows_out[0].peer(s)} for s in range(1, N_SX)] + to_x + to_y
+    greeted += [onward[0], onward[4], backward[0], backward[4]]
     barrier = pltpu.get_barrier_semaphore()
     for target in greeted:
         pl.semaphore_signal(barrier, inc=1, device_id=target, device_id_type=MESH)
@@ -271,13 +297,6 @@
     for piece in (1, 2, 0, 4, 3):
         halo(piece, True).start()
 
-    def tell(r):
-        for step in (2**r, N_SX - 2**r):
-            peer = {"sx": lax.rem(me + step, N_SX)}
-            pl.semaphore_signal(near.at[r], inc=1, device_id=peer, device_id_type=MESH)
-
-    tell(0)
-
     ids = ids_ref[...]
     named = lax.broadcasted_iota(jnp.int32, (32, 512), 0) == ids
     earlier = lax.broadcasted_iota(jnp.int32, (512, 512), 0) < lax.broadcasted_iota(
@@ -290,21 +309,15 @@
     for c in range(4):
         here = (lax.broadcasted_iota(jnp.int32, (256, 512), 0) + 256 * c).astype(F32)
         place[256 * c : 256 * c + 256] = jnp.where(here == slot, 1.0, 0.0).astype(BF16)
-    pl.semaphore_wait(near.at[0], 2)
-    tell(1)
 
     def gather(e, rows_ref, out_ref):
         rows = dot(place[512 * e : 512 * e + 512], rows_ref[...]).astype(BF16)
         out_ref[e] = rows.reshape(N_SX, CAP, 512)
 
     gather(0, cot_ref, csend)
-    pl.semaphore_wait(near.at[1], 2)
-    tell(2)
     gather(1, cot_ref, csend)
-    pl.semaphore_wait(near.at[2], 2)
+    cots_out.start()
     for e in range(2):
-        for s in range(1, N_SX):
-            cots_out.copy(s, e).start()
         cotr[e, 0] = csend[e, me]
 
     lane = lax.shift_right_logical(lax.broadcasted_iota(jnp.int32, (256, 128), 1), 5)
@@ -349,19 +362,15 @@
         normed2[128 * c : 128 * c + 128] = rows.astype(BF16)
     for e in range(2):
         gather(e, normed2, send)
-        for s in range(1, N_SX):
-            rows_out.copy(s, e).start()
+        rows_out[e].start()
         recv[e, 0] = send[e, me]
     loads[2].wait()
     loads[3].wait()
-    for e in range(2):
-        for s in range(1, N_SX):
-            cots_out.copy(s, e).wait_send()
+    cots_out.wait(csend.at[:, others], cs.at[0])
+    cots_out.wait(cotr.at[:, others], cr.at[0])
 
     def hidden_part(e):
-        for s in range(1, N_SX):
-            cots_out.copy(s, e).wait_recv()
-            rows_out.copy(s, e).wait_recv()
+        rows_out[e].wait(recv.at[e, others], xr.at[e])
         rows = recv[e].reshape(512, 512)
         logits = dot_nt(rows, router_ref[...])
         column = lax.broadcasted_iota(jnp.int32, logits.shape, 1) == 2 * me + e
@@ -375,7 +384,11 @@
             hid, slope = gelu_parts(act)
             hidden[e, :, part] = hid.astype(BF16)
             through = dot_nt(rgrad[e], wdown[e, part, :])
-            gact[e, :, part] = (through * slope).astype(BF16)
+            grad = (through * slope).astype(BF16)
+            for n in range(2):
+                col = (lax.rem(f, 2) * 2 + n) * 512 + (f // 2) * 128
+                col = pl.multiple_of(col, 128)
+                gact[e, :, pl.ds(col, 128)] = grad[:, 128 * n : 128 * n + 128]
             return carry
 
         lax.fori_loop(0, 8, step, 0)
@@ -383,77 +396,71 @@
     def return_part(e):
         out = dot(hidden[e], wdown[e]).astype(BF16)
         csend[e] = out.reshape(N_SX, CAP, 512)
-        for s in range(1, N_SX):
-            home.copy(s, e).start()
         back[e, me] = csend[e, 0]
 
+    def x_of(q):
+        return (q % 2) * 2 + q // 2
+
     def halves_of(e):
-        def columns(ix, iy):
-            return pl.ds(pl.multiple_of(shard_of(ix, iy) * 128, 128), 128)
-
-        def up_full(ix, iy):
-            return dot(rows_t[e], gact[e, :, columns(ix, iy)])
-
-        def up_part(h, ix, iy):
-            return dot(rows_t[e, 256 * h : 256 * h + 256], gact[e, :, columns(ix, iy)])
-
-        def down_full(iy, ix):
-            return dot_tn(hidden[e, :, columns(ix, iy)], rgrad[e])
-
-        def down_part(h, iy, ix):
-            return dot_tn(hidden[e, :, columns(ix, iy)], rgrad[e, :, 256 * h : 256 * h + 256])
+        def fill_up(to, ix, rank_of):
+            q = lax.rem(ix, 2) * 2 + ix // 2
+            all_y = dot(rows_t[e], gact[e, :, pl.ds(pl.multiple_of(q * 512, 512), 512)])
+            for iy in range(4):
+                for h in range(2):
+                    part = all_y[256 * h : 256 * h + 256, 128 * iy : 128 * iy + 128]
+                    to[h, rank_of(iy)] = part.astype(BF16)
+
+        def fill_down(to, iy, rank_of):
+            hid = hidden[e, :, pl.ds(pl.multiple_of(iy * 512, 512), 512)]
+            all_x = dot_tn(hid, rgrad[e])
+            for q in range(4):
+                for h in range(2):
+                    part = all_x[128 * q : 128 * q + 128, 256 * h : 256 * h + 256]
+                    to[h, rank_of(x_of(q))] = part.astype(BF16)
 
         up_refs = [ref.at[e] for ref in (us, u1, u2, uh) + sems[:4]]
         down_refs = [ref.at[e] for ref in (ds, d1, d2, dh) + sems[4:]]
         return (
             RingHalf(
-                up_full, up_part, lambda v, h: v[256 * h : 256 * h + 256],
-                x, y, to_x, to_y, up_refs, lambda h: oup_ref.at[e, pl.ds(256 * h, 256)],
+                fill_up, x, y, to_x, to_y, up_refs, lambda h: oup_ref.at[e, pl.ds(256 * h, 256)]
             ),
             RingHalf(
-                down_full, down_part, lambda v, h: v[:, 256 * h : 256 * h + 256],
-                y, x, to_y, to_x, down_refs, lambda h: odown_ref.at[e, :, pl.ds(256 * h, 256)],
+                fill_down, y, x, to_y, to_x, down_refs,
+                lambda h: odown_ref.at[e, :, pl.ds(256 * h, 256)],
             ),
         )
 
     first, second = halves_of(0), halves_of(1)
 
-    def each(halves, method):
-        def step(k, carry):
+    def each(halves, method, *steps):
+        for step in steps or ((),):
             for half in halves:
-                getattr(half, method)(k)
-            return carry
-
-        lax.fori_loop(0, 4, step, 0)
-
-    def close(halves):
-        for k in range(4):
-            for half in halves:
-                half.close1(k)
+                getattr(half, method)(*step)
 
     hidden_part(0)
-    each(first, "send_own")
-    each(first, "pass_on")
+    each(first, "send_far")
+    each(first, "send_raw")
+    each(first, "pass_on", (0,), (1,))
+    each(first, "keep_own")
     hidden_part(1)
-    each(second, "send_own")
-    close(first)
+    each(second, "send_far")
+    each(second, "send_raw")
+    each(first, "close1", (0,), (1,))
     return_part(0)
     return_part(1)
-    each(second, "pass_on")
-    for half in first:
-        half.pass_on2()
-    close(second)
-    for half in second:
-        half.pass_on2()
+    home.start()
+    each(second, "pass_on", (0,), (1,))
+    each(first, "pass_on2")
+    each(second, "keep_own")
+    each(second, "close1", (0,), (1,))
+    each(second, "pass_on2")
     logits = dot_nt(router_ref[...], normed2[...])
     gate = jax.nn.sigmoid(jnp.sum(jnp.where(named, logits, 0.0), axis=0, keepdims=True))
     same_token = lax.broadcasted_iota(jnp.int32, (512, 512), 0) == lax.broadcasted_iota(
         jnp.int32, (512, 512), 1
     )
     gate = jnp.sum(jnp.where(same_token, gate, 0.0), axis=1, keepdims=True)
-    for e in range(2):
-        for s in range(1, N_SX):
-            home.copy(s, e).wait_recv()
+    home.wait(back.at[:, others], br.at[0])
     moe = dot_tn(place[...], back[...].reshape(1024, 512))
     mixed_ref[...] = (resid[...].reshape(512, 512) + gate * moe).astype(BF16)
     for half in first + second:
@@ -461,9 +468,8 @@
     for half in first + second:
         half.finish()
     for e in range(2):
-        for s in range(1, N_SX):
-            rows_out.copy(s, e).wait_send()
-            home.copy(s, e).wait_send()
+        rows_out[e].wait(send.at[e, others], xs.at[e])
+    home.wait(csend.at[:, others], bs.at[0])
     for piece in range(5):
         halo(piece, True).wait_send()
         halo(piece, False).wait_send()
@@ -473,7 +479,7 @@
     dma = pltpu.SemaphoreType.DMA
     vmem = pl.BlockSpec(memory_space=pltpu.VMEM)
     anywhere = pl.BlockSpec(memory_space=pl.ANY)
-    ring = [dma((2, 3, 2, 4)), dma((2, 3, 2, 4)), dma((2, 3, 2)), dma((2, 3, 2))]
+    ring = [dma((2,)), dma((2, 3, 2, 2)), dma((2,)), dma((2, 3, 2))]
     buffers = [
         ((512, 1536), BF16),
         ((512, 512), BF16),
@@ -497,11 +503,11 @@
         ((2, 512, 2048), BF16),
         ((2, 512, 2048), BF16),
         ((2, N_SX, CAP, 512), BF16),
-        ((2, 2, 2, 4, 256, 128), BF16),
+        ((2, 4, 2, 4, 256, 128), BF16),
         ((2, 3, 2, 4, 256, 128), BF16),
         ((2, 3, 2, 256, 128), BF16),
         ((2, 3, 2, 256, 128), BF16),
-        ((2, 2, 2, 4, 128, 256), BF16),
+        ((2, 4, 2, 4, 128, 256), BF16),
         ((2, 3, 2, 4, 128, 256), BF16),
         ((2, 3, 2, 128, 256), BF16),
         ((2, 3, 2, 128, 256), BF16),
@@ -516,9 +522,9 @@
         in_specs=[vmem] * 3 + [pl.BlockSpec(memory_space=pltpu.SMEM), vmem] + [anywhere] * 4,
         out_specs=(vmem,) * 3,
         scratch_shapes=[pltpu.VMEM(shape, kind) for shape, kind in buffers]
-        + [dma((4,)), pltpu.SemaphoreType.REGULAR((3,))]
+        + [dma((4,))]
         + [dma((5,))] * 4
-        + [dma((2, N_SX))] * 6
+        + [dma((2,))] * 6
         + ring * 2,
         compiler_params=pltpu.CompilerParams(
             collective_id=0, has_side_effects=True, vmem_limit_bytes=VMEM_MIB * 1024 * 1024

time: 129 us -> 117 us (0.907)
  Pallas kernels: 123 us -> 112 us
    pallas_call x1, Pallas kernels: 123 us -> 112 us  [on_device(): pl.pallas_call(block_kernel, out_shape=(jax.ShapeDtypeStruct((512, 512),...]
where the time goes in v5:
time: 117 us
  Pallas kernels  112 us (96%)
  local copies, waits for them, and re-layouts  4.47 us (4%)
    pallas_call x1, Pallas kernels, on_device(): pl.pallas_call(block_kernel, out_shape=(jax.ShapeDtypeStruct((512, 512),...  112 us
    unnamed x9, local copies, waits for them, and re-layouts  4.47 us

profile of v5, /device:TPU:1, one launch (start us, length us, event | category | flops | bytes accessed | tf_op | source)
XLA Modules:
  0.0 116.8 jit_solution(8387860800803397483)
XLA Ops:
  0.6 0.0 copy-start
  0.6 0.7 copy-done
  1.4 0.0 copy-start.1
  1.4 0.7 copy-done.1
  2.1 0.0 copy-start.2
  2.1 0.7 copy-done.2
  2.7 111.7 %block.1 = (bf16[512,512]{1,0:T(8,128)(2,1)S(1)}, f32[2,512,128]{2,1,0:T(8,128)S(1)}, f32[2,128,512]{2,1,0:T(8,128)S(1)}) custom-call(bf16[16,32,512]{2,1,0:T(8,128)(2,1)} %bitcast.8, bf16[512,512]{1,0:T(8,128)(2,1)} %bitcast.9, s32[1,512]{1,0:T(1,128)S(1)} %bitcast.7, f32[16]{0:T(128)S(1)} %copy-done.2, bf16[32,512]{1,0:T(8,128)(2,1)S(1)} %bitcast.6, ...), custom_call_target="tpu_custom_call" | custom-call | tf_op jit(solution)/shard_map/block/pallas_call | solution.py:515
  114.4 0.8 copy.15
  115.2 0.8 copy.16
  116.0 0.8 copy.17
Async XLA Ops:
  0.6 0.8 copy-start
  1.4 0.7 copy-start.1
  2.1 0.7 copy-start.2

commit v6 on v5

--- a/solution.py
+++ b/solution.py
@@ -224,9 +224,9 @@
 
 
 def block_kernel(
-    tok_ref, cot_ref, ids_ref, scale_ref, router_ref, wqkv_any, wproj_any, wup_any, wdown_any,
+    tok_any, cot_any, ids_any, scale_any, router_any, wqkv_any, wproj_any, wup_any, wdown_any,
     mixed_ref, oup_ref, odown_ref,
-    wqkv, wproj, wup, wdown,
+    tok_ref, cot_ref, ids_ref, scale_ref, router_ref, wqkv, wproj, wup, wdown,
     resid, nsend, region, qkv, joined, attb, homeb, place, normed2,
     send, csend, recv, cotr, rgrad, rows_t, hidden, gact, back,
     us, u1, u2, uh, ds, d1, d2, dh,
@@ -259,20 +259,27 @@
     for target in greeted:
         pl.semaphore_signal(barrier, inc=1, device_id=target, device_id_type=MESH)
 
-    loads = [
-        pltpu.make_async_copy(wqkv_any, wqkv, wsem.at[0]),
-        pltpu.make_async_copy(wproj_any, wproj, wsem.at[1]),
-        pltpu.make_async_copy(wup_any, wup, wsem.at[2]),
-        pltpu.make_async_copy(wdown_any, wdown, wsem.at[3]),
-    ]
-    for load in loads:
-        load.start()
+    pairs = (
+        (wqkv_any, wqkv),
+        (wproj_any, wproj),
+        (wup_any, wup),
+        (wdown_any, wdown),
+        (tok_any, tok_ref),
+        (ids_any, ids_ref),
+        (cot_any, cot_ref),
+        (scale_any, scale_ref),
+        (router_any, router_ref),
+    )
+    loads = [pltpu.make_async_copy(a, b, wsem.at[n]) for n, (a, b) in enumerate(pairs)]
+    for n in (4, 5, 6, 7, 8, 0, 1, 2, 3):
+        loads[n].start()
 
     places = ((1, 0), (2, 0), (3, 0), (0, 1), (0, 0))
 
     def tile_at(cg, rh):
         return (slice(8 * rh, 8 * rh + 8), slice(8 * cg, 8 * cg + 8))
 
+    loads[4].wait()
     resid[...] = tok_ref[...].astype(F32)
     for piece, (cg, rh) in enumerate(places):
         from_cg, from_rh = (cg + 3) % 4, 1 - rh
@@ -297,6 +304,7 @@
     for piece in (1, 2, 0, 4, 3):
         halo(piece, True).start()
 
+    loads[5].wait()
     ids = ids_ref[...]
     named = lax.broadcasted_iota(jnp.int32, (32, 512), 0) == ids
     earlier = lax.broadcasted_iota(jnp.int32, (512, 512), 0) < lax.broadcasted_iota(
@@ -314,6 +322,7 @@
         rows = dot(place[512 * e : 512 * e + 512], rows_ref[...]).astype(BF16)
         out_ref[e] = rows.reshape(N_SX, CAP, 512)
 
+    loads[6].wait()
     gather(0, cot_ref, csend)
     gather(1, cot_ref, csend)
     cots_out.start()
@@ -326,8 +335,8 @@
     )
     ones = jnp.where(lane == row, 1.0, 0.0).astype(BF16)
 
-    loads[0].wait()
-    loads[1].wait()
+    for n in (0, 1, 7, 8):
+        loads[n].wait()
     row_cut = jnp.where(sy == 0, 1, 0)
     for w in (1, 0):
         for piece in (1, 2) if w else (0, 4, 3):
@@ -362,6 +371,8 @@
         normed2[128 * c : 128 * c + 128] = rows.astype(BF16)
     for e in range(2):
         gather(e, normed2, send)
+        if e:
+            rows_out[0].wait(send.at[0, others], xs.at[0])
         rows_out[e].start()
         recv[e, 0] = send[e, me]
     loads[2].wait()
@@ -467,8 +478,7 @@
         half.close2()
     for half in first + second:
         half.finish()
-    for e in range(2):
-        rows_out[e].wait(send.at[e, others], xs.at[e])
+    rows_out[1].wait(send.at[1, others], xs.at[1])
     home.wait(csend.at[:, others], bs.at[0])
     for piece in range(5):
         halo(piece, True).wait_send()
@@ -478,9 +488,14 @@
 def on_device(tokens, cotangent, w_qkv, w_proj, logit_scale, w_router, w_up, w_down, expert_ids):
     dma = pltpu.SemaphoreType.DMA
     vmem = pl.BlockSpec(memory_space=pltpu.VMEM)
-    anywhere = pl.BlockSpec(memory_space=pl.ANY)
+    hbm = pl.BlockSpec(memory_space=pltpu.HBM)
     ring = [dma((2,)), dma((2, 3, 2, 2)), dma((2,)), dma((2, 3, 2))]
     buffers = [
+        ((16, 32, 512), BF16),
+        ((512, 512), BF16),
+        ((1, 512), jnp.int32),
+        None,
+        ((32, 512), BF16),
         ((512, 1536), BF16),
         ((512, 512), BF16),
         ((2, 512, 2048), BF16),
@@ -519,10 +534,10 @@
             jax.ShapeDtypeStruct((2, 512, 128), F32),
             jax.ShapeDtypeStruct((2, 128, 512), F32),
         ),
-        in_specs=[vmem] * 3 + [pl.BlockSpec(memory_space=pltpu.SMEM), vmem] + [anywhere] * 4,
+        in_specs=[hbm] * 9,
         out_specs=(vmem,) * 3,
-        scratch_shapes=[pltpu.VMEM(shape, kind) for shape, kind in buffers]
-        + [dma((4,))]
+        scratch_shapes=[pltpu.VMEM(*b) if b else pltpu.SMEM((16,), F32) for b in buffers]
+        + [dma((9,))]
         + [dma((5,))] * 4
         + [dma((2,))] * 6
         + ring * 2,

time: 117 us -> 112 us (0.957); the launches traced: 117 us -> 110 us
  Pallas kernels: 112 us -> 105 us
    pallas_call x1, Pallas kernels: 112 us -> 105 us  [on_device(): pl.pallas_call(block_kernel, out_shape=(jax.ShapeDtypeStruct((512, 512),...]
where the time goes in v6:
time: 112 us; the launch traced here: 110 us
  Pallas kernels  105 us (94%)
  local copies, waits for them, and re-layouts  4.47 us (4%)
    pallas_call x1, Pallas kernels, on_device(): pl.pallas_call(block_kernel, out_shape=(jax.ShapeDtypeStruct((512, 512),...  105 us
    unnamed x9, local copies, waits for them, and re-layouts  4.47 us

profile of v6, /device:TPU:1, one launch (start us, length us, event | category | flops | bytes accessed | tf_op | source)
XLA Modules:
  0.0 110.4 jit_solution(16760901277991656731)
XLA Ops:
  0.6 0.0 copy-start
  0.6 0.7 copy-done
  1.4 0.0 copy-start.1
  1.4 0.7 copy-done.1
  2.1 0.0 copy-start.2
  2.1 0.7 copy-done.2
  2.7 105.3 %block.1 = (bf16[512,512]{1,0:T(8,128)(2,1)S(1)}, f32[2,512,128]{2,1,0:T(8,128)S(1)}, f32[2,128,512]{2,1,0:T(8,128)S(1)}) custom-call(bf16[16,32,512]{2,1,0:T(8,128)(2,1)} %bitcast.8, bf16[512,512]{1,0:T(8,128)(2,1)} %bitcast.9, s32[1,512]{1,0:T(1,128)S(1)} %bitcast.7, f32[16]{0:T(128)S(1)} %copy-done.2, bf16[32,512]{1,0:T(8,128)(2,1)S(1)} %bitcast.6, ...), custom_call_target="tpu_custom_call" | custom-call | tf_op jit(solution)/shard_map/block/pallas_call | solution.py:530
  108.0 0.8 copy.15
  108.8 0.8 copy.16
  109.6 0.8 copy.17
Async XLA Ops:
  0.6 0.8 copy-start
  1.4 0.7 copy-start.1
  2.1 0.7 copy-start.2

commit v7 on v6

--- a/solution.py
+++ b/solution.py
@@ -453,11 +453,11 @@
     each(first, "send_raw")
     each(first, "pass_on", (0,), (1,))
     each(first, "keep_own")
+    return_part(0)
     hidden_part(1)
     each(second, "send_far")
     each(second, "send_raw")
     each(first, "close1", (0,), (1,))
-    return_part(0)
     return_part(1)
     home.start()
     each(second, "pass_on", (0,), (1,))

time: 112 us -> 111 us (level)
  no operation moved by 1% of the time
where the time goes in v7:
time: 111 us; the launch traced here: 110 us
  Pallas kernels  105 us (95%)
  local copies, waits for them, and re-layouts  4.47 us (4%)
    pallas_call x1, Pallas kernels, on_device(): pl.pallas_call(block_kernel, out_shape=(jax.ShapeDtypeStruct((512, 512),...  105 us
    unnamed x9, local copies, waits for them, and re-layouts  4.47 us

profile of v7, /device:TPU:1, one launch (start us, length us, event | category | flops | bytes accessed | tf_op | source)
XLA Modules:
  0.0 109.7 jit_solution(12679468130154828732)
XLA Ops:
  0.6 0.0 copy-start
  0.6 0.7 copy-done
  1.4 0.0 copy-start.1
  1.4 0.7 copy-done.1
  2.1 0.0 copy-start.2
  2.1 0.7 copy-done.2
  2.7 104.5 %block.1 = (bf16[512,512]{1,0:T(8,128)(2,1)S(1)}, f32[2,512,128]{2,1,0:T(8,128)S(1)}, f32[2,128,512]{2,1,0:T(8,128)S(1)}) custom-call(bf16[16,32,512]{2,1,0:T(8,128)(2,1)} %bitcast.8, bf16[512,512]{1,0:T(8,128)(2,1)} %bitcast.9, s32[1,512]{1,0:T(1,128)S(1)} %bitcast.7, f32[16]{0:T(128)S(1)} %copy-done.2, bf16[32,512]{1,0:T(8,128)(2,1)S(1)} %bitcast.6, ...), custom_call_target="tpu_custom_call" | custom-call | tf_op jit(solution)/shard_map/block/pallas_call | solution.py:530
  107.3 0.8 copy.15
  108.1 0.8 copy.16
  108.9 0.8 copy.17
Async XLA Ops:
  0.6 0.8 copy-start
  1.4 0.7 copy-start.1
  2.1 0.7 copy-start.2
